TPU v7x, 512 devices: a whole 4x8x8 slice. The times are simulated.
512 devices in a mesh: row: 16 (over y_hi, x, core), col: 32 (over y_lo, z).
Axes of the slice: x: 4, y: 8 (y_hi: 2, y_lo: 4; y = y_hi * 4 + y_lo), z: 8, core: 2. Of those that a mesh axis runs over, the one named last changes fastest.
Arguments:
- density: bfloat16 [2, 12288, 12288], P(None, 'row', 'col'), may hold values from -6 to 6
- hcols: int32 [96, 4], P('row'), may hold values from -1 to 95, as said below
- hvals: bfloat16 [96, 4, 128, 128], P('row'), may hold values from -0.25 to 0.25
Outputs:
- propagated: float32 [2, 12288, 12288], P(None, 'row', 'col')
Inputs may be any that keep to these rules, and one draw needn't show every extreme that they name: In block row b the first slots of hcols hold b and then, in increasing order, some of b + 1 to b + 3, all below 96; the remaining slots hold -1.
All inputs are finite; a program needn't handle non-finite values.
Results may differ from a plain program's by a relative error of at most 0.0022.
Values may be sent and summed in bfloat16 or wider, within the bound.
No kernel may reach another device: no remote copies, remote signals or barrier semaphores. Data moves between devices by JAX's collectives and lax.ppermute only.
A program may use at most 128 MiB of HBM per device.

v0:
```python
import jax
import jax.numpy as jnp
from jax import lax
from jax.sharding import PartitionSpec as P

BLK = 128
BAND = 3


DT = 0.5


def passed_along(block, axis, distance):
    devices = range(lax.axis_size(axis))
    route = [(i - distance, i) for i in devices if i - distance in devices]
    return lax.ppermute(block, axis, route)


def broadcast(block, axis, holder):
    block = jnp.where(lax.axis_index(axis) == holder, block, jnp.zeros_like(block))
    return lax.psum(block, axis)


def padded_2(shard, sides, width):
    for axis, dim in sides:
        count, length = (lax.axis_size(axis), shard.shape[dim])
        up = [(i, (i + 1) % count) for i in range(count - 1)]
        down = [(j, i) for i, j in up]
        last = lax.slice_in_dim(shard, length - width, length, axis=dim)
        leading = lax.slice_in_dim(shard, 0, width, axis=dim)
        before = lax.ppermute(last, axis, up)
        after = lax.ppermute(leading, axis, down)
        shard = jnp.concatenate([before, shard, after], axis=dim)
    return shard


def band_blocks(upper, lower):
    count = upper.shape[0]
    ext = jnp.concatenate([lower, upper], axis=0)
    pieces = []
    for q in range(2 * BAND + 1):
        offset = q - BAND
        if offset > 0:
            pieces.append(ext[BAND:, offset])
        elif offset < 0:
            pieces.append(jnp.swapaxes(ext[BAND + offset : BAND + offset + count, -offset], 1, 2))
        else:
            diag = ext[BAND:, 0].astype(jnp.float32)
            pieces.append((diag + jnp.swapaxes(diag, 1, 2)).astype(jnp.bfloat16))
    return jnp.stack(pieces, axis=1)


def column_windows(spread_field, column_band, height, width, cols_here):
    stacked = jnp.stack(
        [spread_field[:, :, q * BLK : q * BLK + width] for q in range(2 * BAND + 1)], axis=2
    )
    stacked = stacked.reshape(2, height, 2 * BAND + 1, cols_here, BLK)
    product = jnp.einsum(
        "piqjy,jqxy->pijx", stacked, column_band, preferred_element_type=jnp.float32
    )
    return product.reshape(2, height, width)


def on_device(density, hcols, hvals):
    rows_here = hvals.shape[0]
    first = lax.axis_index("row") * rows_here
    row_ids = first + jnp.arange(rows_here, dtype=jnp.int32)
    targets = row_ids[:, None] + jnp.arange(BAND + 1, dtype=jnp.int32)[None, :]
    onehot = (hcols[:, None, :] == targets[:, :, None]).astype(jnp.bfloat16)
    upper = jnp.einsum("bps,bsxy->bpxy", onehot, hvals, preferred_element_type=jnp.float32).astype(
        jnp.bfloat16
    )
    lower = passed_along(upper[rows_here - BAND :], "row", 1)
    band = band_blocks(upper, lower)
    half_rows = rows_here // 2
    column_index = lax.axis_index("col")
    mine = lax.dynamic_slice_in_dim(band, column_index % 2 * half_rows, half_rows, 0)
    column_band = broadcast(mine, "row", column_index // 2)
    margin = BAND * BLK

    def rate(field):
        height = field.shape[1]
        width = field.shape[2]
        cols_here = width // BLK
        tall = padded_2(field, (("row", 1),), margin)
        stacked = jnp.stack(
            [tall[:, q * BLK : q * BLK + height] for q in range(2 * BAND + 1)], axis=1
        )
        stacked = stacked.reshape(2, 2 * BAND + 1, rows_here, BLK, width)
        left = jnp.einsum("bqxy,pqbyz->pbxz", band, stacked, preferred_element_type=jnp.float32)
        left = left.reshape(2, height, width)
        padded = jnp.pad(field, ((0, 0), (0, 0), (margin, margin)))
        right = column_windows(padded, column_band, height, width, cols_here)
        blocks = field.reshape(2, height, cols_here, BLK)
        low_terms = []
        high_terms = []
        for edge in range(BAND):
            low_total = jnp.zeros((2, height, BLK), jnp.float32)
            for k in range(edge + 1):
                low_total = low_total + jnp.einsum(
                    "piy,yx->pix",
                    blocks[:, :, k],
                    column_band[k, edge - k],
                    preferred_element_type=jnp.float32,
                )
            low_terms.append(low_total)
            high_total = jnp.zeros((2, height, BLK), jnp.float32)
            for m in range(edge, BAND):
                k = cols_here - BAND + m
                high_total = high_total + jnp.einsum(
                    "piy,yx->pix",
                    blocks[:, :, k],
                    column_band[k, edge - m + 2 * BAND],
                    preferred_element_type=jnp.float32,
                )
            high_terms.append(high_total)
        low_edge = jnp.stack(low_terms, axis=2).reshape(2, height, margin)
        high_edge = jnp.stack(high_terms, axis=2).reshape(2, height, margin)
        from_right = passed_along(low_edge, "col", -1)
        from_left = passed_along(high_edge, "col", 1)
        right = right.at[:, :, width - margin :].add(from_right)
        right = right.at[:, :, :margin].add(from_left)
        commutator = left - right
        return jnp.stack([commutator[1], -commutator[0]])

    start = density.astype(jnp.float32)
    first_rate = rate(density)
    middle = (start + DT * first_rate).astype(jnp.bfloat16)
    second_rate = rate(middle)
    return start + DT / 2 * (first_rate + second_rate)


def solution(mesh):
    placed = (P(None, "row", "col"), P("row", None), P("row", None, None, None))
    return jax.shard_map(
        on_device, mesh=mesh, in_specs=placed, out_specs=P(None, "row", "col"), check_vma=False
    )
```

profile of v0, /device:TPU:15, one launch (start us, length us, event | category | flops | bytes accessed | tf_op | source)
XLA Modules:
  0.0 446.9 jit_solution(2666298044236028428)
XLA Ops:
  6.5 2.5 fusion.98
  9.0 7.2 %collective-permute-start = (bf16[2,384,384]{2,1,0:T(8,128)(2,1)}, bf16[2,384,384]{2,1,0:T(8,128)(2,1)}, u32[]{:S(2)}, u32[]{:S(2)}) collective-permute-start(bf16[2,384,384]{2,1,0:T(8,128)(2,1)} %get-tuple-element.121), channel_id=1, source_target_pairs={{0,32},{32,64},{64,96},{96,128},{128,160},{160,192},{192,224},{224... | collective-permute-start | bytes 1769480 | tf_op jit(solution)/shard_map/ppermute | solution.py:31
  16.2 1.9 collective-permute-start.1
  19.2 9.7 %collective-permute-start.2 = (bf16[3,4,128,128]{3,1,2,0:T(4,128)(2,1)S(1)}, bf16[3,4,128,128]{3,1,2,0:T(4,128)(2,1)}, u32[]{:S(2)}, u32[]{:S(2)}) collective-permute-start(bf16[3,4,128,128]{3,1,2,0:T(4,128)(2,1)S(1)} %slice.335), channel_id=1, source_target_pairs={{0,32},{32,64},{64,96},{96,128},{128,160},{160,192},{192,224},{224... | collective-permute-start | bytes 1179656 | tf_op jit(solution)/shard_map/ppermute | solution.py:16
  28.9 1.3 slice.341
  33.2 2.4 pad_slice_fusion.4
  35.6 2.4 copy.330
  38.0 2.4 copy.331
  40.4 1.4 copy.332
  41.8 2.4 copy.333
  44.2 2.4 copy.334
  46.6 2.6 constant_dynamic-update-slice_fusion.15
  49.2 1.3 constant_dynamic-update-slice_fusion.14
  55.4 3.6 pad_maximum_fusion.7
  60.0 2.0 copy_bitcast_fusion
  62.1 1.9 copy.323
  64.0 1.9 copy.324
  68.2 7.8 %stack.174 = bf16[6,7,128,128]{3,1,2,0:T(8,128)(2,1)} concatenate(bf16[6,1,128,128]{3,1,2,0:T(2,128)(2,1)} %copy.322, bf16[6,1,128,128]{3,1,2,0:T(2,128)(2,1)} %copy.323, bf16[6,1,128,128]{3,1,2,0:T(2,128)(2,1)} %copy.324, bf16[6,1,128,128]{3,1,2,0:T(2,128)(2,1)S(1)} %copy.325, bf16[6,3,128,128]{3,1,2,0:T(4,128)(2,1)S(1)} %copy-done.25), dimensions={1} | concatenate | bytes 2752512 | tf_op jit(solution)/shard_map/stack | solution.py:50
  76.0 2.1 dynamic-slice_select_fusion
  84.4 178.2 %all-reduce.4.cloned.1.call-done = bf16[3,7,128,128]{3,1,2,0:T(8,128)(2,1)} async-done(((bf16[3,7,128,128]{3,1,2,0:T(8,128)(2,1)}), bf16[3,7,128,128]{3,1,2,0:T(8,128)(2,1)}) %all-reduce.4.cloned.1.call-update) | async-done | bytes 688144 | tf_op jit(solution)/shard_map/psum | solution.py:21
  262.6 2.8 fusion.99
  267.6 1.6 copy.356
  269.2 3.2 copy.357
  272.4 3.4 collective-permute-start.4
  277.9 1.6 copy.347
  279.4 3.0 copy.348
  282.5 4.1 collective-permute-start.3
  286.6 2.0 constant_dynamic-update-slice_fusion.2
  294.4 4.9 %fusion.6 = f32[2,6,128,384]{3,2,0,1:T(8,128)S(1)} fusion(bf16[2,7,6,128,384]{4,3,2,0,1:T(8,128)(2,1)} %constant_dynamic-update-slice_fusion.4, bf16[6,7,128,128,1]{3,1,2,0,4:T(8,128)(2,1)S(1)} %bitcast.347), kind=kOutput, calls=%fused_computation.32 | convolution fusion | flops 1056964608 | bytes 11993088 | tf_op jit(solution)/shard_map/bqxy,pqbyz->pbxz/dot_general | solution.py:90
  299.3 1.6 copy.327
  300.9 2.7 convolution_bitcast_fusion.1
  303.6 1.8 copy.336
  305.4 3.0 copy.349
  308.4 18.9 %collective-permute-done.4 = f32[2,768,384]{2,1,0:T(8,128)} collective-permute-done((f32[2,768,384]{2,1,0:T(8,128)}, f32[2,768,384]{2,1,0:T(8,128)}, u32[]{:S(2)}, u32[]{:S(2)}) %collective-permute-start.4) | collective-permute-done | bytes 2359328 | tf_op jit(solution)/shard_map/ppermute | solution.py:16
  327.4 8.6 %collective-permute-done.3 = f32[2,768,384]{2,1,0:T(8,128)} collective-permute-done((f32[2,768,384]{2,1,0:T(8,128)}, f32[2,768,384]{2,1,0:T(8,128)}, u32[]{:S(2)}, u32[]{:S(2)}) %collective-permute-start.3) | collective-permute-done | bytes 2359328 | tf_op jit(solution)/shard_map/ppermute | solution.py:16
  336.0 4.2 bitcast_subtract_fusion.1
  348.7 1.9 collective-permute-start.6
  350.6 9.7 %collective-permute-start.5 = (bf16[2,384,384]{2,1,0:T(8,128)(2,1)}, bf16[2,384,384]{2,1,0:T(8,128)(2,1)}, u32[]{:S(2)}, u32[]{:S(2)}) collective-permute-start(bf16[2,384,384]{2,1,0:T(8,128)(2,1)} %get-tuple-element.112), channel_id=1, source_target_pairs={{0,32},{32,64},{64,96},{96,128},{128,160},{160,192},{192,224},{224... | collective-permute-start | bytes 1769480 | tf_op jit(solution)/shard_map/ppermute | solution.py:31
  361.5 1.6 copy.398
  363.1 3.2 copy.399
  366.2 2.1 collective-permute-start.8
  368.3 1.5 convolution_add_fusion.4
  369.8 2.0 fusion.14
  371.8 1.4 copy.374
  376.0 1.6 copy.389
  377.5 3.1 copy.390
  380.6 6.0 %collective-permute-start.7 = (f32[2,768,384]{2,1,0:T(8,128)}, f32[2,768,384]{2,1,0:T(8,128)}, u32[]{:S(2)}, u32[]{:S(2)}) collective-permute-start(f32[2,768,384]{2,1,0:T(8,128)} %copy.390), channel_id=1, source_target_pairs={{1,0},{2,1},{3,2},{4,3},{5,4},{6,5},{7,6},{8,7},{9,8},{10,9},{11,1... | collective-permute-start | bytes 7077896 | tf_op jit(solution)/shard_map/ppermute | solution.py:16
  386.6 5.4 %pad_slice_fusion = (bf16[2,768,384]{2,1,0:T(8,128)(2,1)S(1)}, bf16[2,768,384]{2,1,0:T(8,128)(2,1)}, bf16[2,768,384]{2,1,0:T(8,128)(2,1)}, bf16[2,768,384]{2,1,0...) fusion(bf16[2,768,384]{2,1,0:T(8,128)(2,1)S(1)} %fusion.4, ...), kind=kLoop, calls=%fused_computation.4 | loop fusion | flops 14155776 | bytes 14155776 | tf_op jit(solution)/shard_map/slice | solution.py:55
  394.7 1.4 fusion.9
  396.1 1.6 copy.366
  397.7 1.5 copy.367
  399.2 2.4 copy.372
  401.6 2.5 copy.368
  404.1 2.4 copy.373
  406.5 1.4 copy.370
  407.9 2.4 copy.375
  410.3 1.5 copy.371
  411.8 2.4 copy.376
  419.2 1.3 constant_dynamic-update-slice_fusion.23
  421.7 6.1 %convolution_bitcast_fusion = f32[2,768,3,128]{1,3,0,2:T(8,128)S(1)} fusion(bf16[2,768,7,3,128]{4,1,2,0,3:T(8,128)(2,1)} %broadcast_dynamic-update-slice_fusion.2, bf16[3,7,128,128,1]{3,1,2,0,4:T(8,128)(2,1)S(1)} %bitcast.324), kind=kOutput, calls=%fused_computation.34 | convolution fusion | flops 1056964608 | bytes 11304960 | tf_op jit(solution)/shard_map/piqjy,jqxy->pijx/dot_general | solution.py:58
  427.8 1.7 copy.378
  429.5 3.1 copy.391
  432.6 4.2 bitcast_subtract_fusion
  438.4 1.7 convert_add_fusion
  (175 shorter events, 51.2 us)
Async XLA Ops:
  6.5 11.8 %copy-start = (bf16[6,4,128,128]{3,2,1,0:T(8,128)(2,1)S(1)}, bf16[6,4,128,128]{3,2,1,0:T(8,128)(2,1)}, u32[]{:S(2)}) copy-start(bf16[6,4,128,128]{3,2,1,0:T(8,128)(2,1)} %param.21) | copy-start | bytes 2359300
  6.5 11.7 %copy-start.44 = (s32[6,4]{0,1:T(4,128)S(1)}, s32[6,4]{0,1:T(4,128)}, u32[]{:S(2)}) copy-start(s32[6,4]{0,1:T(4,128)} %param.20) | copy-start | bytes 292
  6.5 256.1 %all-reduce.4.cloned.1.call-start = ((), (), s32[]{:S(2)}) async-start(), calls=%async_computation | async-start | bytes 1572864 | tf_op jit(solution)/shard_map/psum | solution.py:21
  9.0 21.2 %copy-start.2 = (bf16[2,768,384]{2,1,0:T(8,128)(2,1)S(1)}, bf16[2,768,384]{2,1,0:T(8,128)(2,1)}, u32[]{:S(2)}) copy-start(bf16[2,768,384]{2,1,0:T(8,128)(2,1)} %param.19) | copy-start | bytes 3538948
  9.0 69.1 %collective-permute-start = (bf16[2,384,384]{2,1,0:T(8,128)(2,1)}, bf16[2,384,384]{2,1,0:T(8,128)(2,1)}, u32[]{:S(2)}, u32[]{:S(2)}) collective-permute-start(bf16[2,384,384]{2,1,0:T(8,128)(2,1)} %get-tuple-element.121), channel_id=1, source_target_pairs={{0,32},{32,64},{64,96},{96,128},{128,160},{160,192},{192,224},{224... | collective-permute-start | bytes 1769480 | tf_op jit(solution)/shard_map/ppermute | solution.py:31
  16.2 270.4 %collective-permute-start.1 = (bf16[2,384,384]{2,1,0:T(8,128)(2,1)}, bf16[2,384,384]{2,1,0:T(8,128)(2,1)}, u32[]{:S(2)}, u32[]{:S(2)}) collective-permute-start(bf16[2,384,384]{2,1,0:T(8,128)(2,1)} %get-tuple-element.120), channel_id=1, source_target_pairs={{32,0},{64,32},{96,64},{128,96},{160,128},{192,160},{224,192},{256... | collective-permute-start | bytes 1769480 | tf_op jit(solution)/shard_map/ppermute | solution.py:32
  19.2 36.2 %collective-permute-start.2 = (bf16[3,4,128,128]{3,1,2,0:T(4,128)(2,1)S(1)}, bf16[3,4,128,128]{3,1,2,0:T(4,128)(2,1)}, u32[]{:S(2)}, u32[]{:S(2)}) collective-permute-start(bf16[3,4,128,128]{3,1,2,0:T(4,128)(2,1)S(1)} %slice.335), channel_id=1, source_target_pairs={{0,32},{32,64},{64,96},{96,128},{128,160},{160,192},{192,224},{224... | collective-permute-start | bytes 1179656 | tf_op jit(solution)/shard_map/ppermute | solution.py:16
  46.6 2.6 copy-start.18
  46.6 3.9 copy-start.15
  49.2 2.5 copy-start.13
  50.5 2.4 copy-start.14
  60.0 8.2 %copy-start.25 = (bf16[6,3,128,128]{3,1,2,0:T(4,128)(2,1)S(1)}, bf16[6,3,128,128]{3,1,2,0:T(4,128)(2,1)}, u32[]{:S(2)}) copy-start(bf16[6,3,128,128]{3,1,2,0:T(4,128)(2,1)} %slice.341) | copy-start | bytes 1769476
  265.4 1.3 copy-start.33
  265.4 1.3 copy-start.40
  265.4 1.3 copy-start.42
  265.5 1.3 copy-start.43
  265.5 1.3 copy-start.31
  265.5 1.6 copy-start.29
  265.5 10.3 %copy-start.38 = (bf16[1,1,128,128]{3,1,2,0:T(2,128)(2,1)}, bf16[1,1,128,128]{3,1,2,0:T(2,128)(2,1)S(1)}, u32[]{:S(2)}) copy-start(bf16[1,1,128,128]{3,1,2,0:T(2,128)(2,1)S(1)} %get-tuple-element.133) | copy-start | bytes 98308
  265.5 10.6 %copy-start.28 = (bf16[1,1,128,128]{3,1,2,0:T(2,128)(2,1)}, bf16[1,1,128,128]{3,1,2,0:T(2,128)(2,1)S(1)}, u32[]{:S(2)}) copy-start(bf16[1,1,128,128]{3,1,2,0:T(2,128)(2,1)S(1)} %get-tuple-element.132) | copy-start | bytes 98308
  265.5 10.9 %copy-start.27 = (bf16[1,1,128,128]{3,1,2,0:T(2,128)(2,1)}, bf16[1,1,128,128]{3,1,2,0:T(2,128)(2,1)S(1)}, u32[]{:S(2)}) copy-start(bf16[1,1,128,128]{3,1,2,0:T(2,128)(2,1)S(1)} %get-tuple-element.131) | copy-start | bytes 98308
  265.5 11.2 %copy-start.36 = (bf16[1,1,128,128]{3,1,2,0:T(2,128)(2,1)}, bf16[1,1,128,128]{3,1,2,0:T(2,128)(2,1)S(1)}, u32[]{:S(2)}) copy-start(bf16[1,1,128,128]{3,1,2,0:T(2,128)(2,1)S(1)} %get-tuple-element.124) | copy-start | bytes 98308
  265.5 11.5 %copy-start.35 = (bf16[1,1,128,128]{3,1,2,0:T(2,128)(2,1)}, bf16[1,1,128,128]{3,1,2,0:T(2,128)(2,1)S(1)}, u32[]{:S(2)}) copy-start(bf16[1,1,128,128]{3,1,2,0:T(2,128)(2,1)S(1)} %get-tuple-element.135) | copy-start | bytes 98308
  265.5 11.8 %copy-start.26 = (bf16[1,1,128,128]{3,1,2,0:T(2,128)(2,1)}, bf16[1,1,128,128]{3,1,2,0:T(2,128)(2,1)S(1)}, u32[]{:S(2)}) copy-start(bf16[1,1,128,128]{3,1,2,0:T(2,128)(2,1)S(1)} %get-tuple-element.134) | copy-start | bytes 98308
  272.4 55.0 %collective-permute-start.4 = (f32[2,768,384]{2,1,0:T(8,128)}, f32[2,768,384]{2,1,0:T(8,128)}, u32[]{:S(2)}, u32[]{:S(2)}) collective-permute-start(f32[2,768,384]{2,1,0:T(8,128)} %copy.357), channel_id=1, source_target_pairs={{0,1},{1,2},{2,3},{3,4},{4,5},{5,6},{6,7},{7,8},{8,9},{9,10},{10,1... | collective-permute-start | bytes 7077896 | tf_op jit(solution)/shard_map/ppermute | solution.py:16
  282.5 53.5 %collective-permute-start.3 = (f32[2,768,384]{2,1,0:T(8,128)}, f32[2,768,384]{2,1,0:T(8,128)}, u32[]{:S(2)}, u32[]{:S(2)}) collective-permute-start(f32[2,768,384]{2,1,0:T(8,128)} %copy.348), channel_id=1, source_target_pairs={{1,0},{2,1},{3,2},{4,3},{5,4},{6,5},{7,6},{8,7},{9,8},{10,9},{11,1... | collective-permute-start | bytes 7077896 | tf_op jit(solution)/shard_map/ppermute | solution.py:16
  288.6 1.9 copy-start.3
  292.0 2.4 copy-start.21
  294.4 6.5 %slice-start = ((s8[8257536]{0:T(1024)(128)(4,1)}), s8[4194304]{0:T(1024)(128)(4,1)S(1)}, s32[]{:S(2)}) async-start(s8[8257536]{0:T(1024)(128)(4,1)} %bitcast.315), calls=%async_computation.1 | async-start | bytes 8388608
  294.4 6.5 %slice-start.1 = ((s8[8257536]{0:T(1024)(128)(4,1)}), s8[4063232]{0:T(1024)(128)(4,1)S(1)}, s32[]{:S(2)}) async-start(s8[8257536]{0:T(1024)(128)(4,1)} %bitcast.315), calls=%async_computation.2 | async-start | bytes 8126464
  299.3 1.6 copy-start.8
  340.3 1.0 copy-start.4
  340.3 1.4 copy-start.6
  343.5 2.4 copy-start.41
  343.5 2.7 copy-start.39
  343.5 4.0 copy-start.37
  344.7 15.5 %copy-start.34 = (bf16[1,1,128,128]{3,1,2,0:T(2,128)(2,1)S(1)}, bf16[1,1,128,128]{3,1,2,0:T(2,128)(2,1)}, u32[]{:S(2)}) copy-start(bf16[1,1,128,128]{3,1,2,0:T(2,128)(2,1)} %copy-done.33) | copy-start | bytes 98308
  346.3 14.3 %copy-start.32 = (bf16[1,1,128,128]{3,1,2,0:T(2,128)(2,1)S(1)}, bf16[1,1,128,128]{3,1,2,0:T(2,128)(2,1)}, u32[]{:S(2)}) copy-start(bf16[1,1,128,128]{3,1,2,0:T(2,128)(2,1)} %copy-done.31) | copy-start | bytes 98308
  347.5 13.4 %copy-start.30 = (bf16[1,1,128,128]{3,1,2,0:T(2,128)(2,1)S(1)}, bf16[1,1,128,128]{3,1,2,0:T(2,128)(2,1)}, u32[]{:S(2)}) copy-start(bf16[1,1,128,128]{3,1,2,0:T(2,128)(2,1)} %copy-done.29) | copy-start | bytes 98308
  348.7 37.9 %collective-permute-start.6 = (bf16[2,384,384]{2,1,0:T(8,128)(2,1)}, bf16[2,384,384]{2,1,0:T(8,128)(2,1)}, u32[]{:S(2)}, u32[]{:S(2)}) collective-permute-start(bf16[2,384,384]{2,1,0:T(8,128)(2,1)} %get-tuple-element.111), channel_id=1, source_target_pairs={{32,0},{64,32},{96,64},{128,96},{160,128},{192,160},{224,192},{256... | collective-permute-start | bytes 1769480 | tf_op jit(solution)/shard_map/ppermute | solution.py:32
  350.6 36.0 %collective-permute-start.5 = (bf16[2,384,384]{2,1,0:T(8,128)(2,1)}, bf16[2,384,384]{2,1,0:T(8,128)(2,1)}, u32[]{:S(2)}, u32[]{:S(2)}) collective-permute-start(bf16[2,384,384]{2,1,0:T(8,128)(2,1)} %get-tuple-element.112), channel_id=1, source_target_pairs={{0,32},{32,64},{64,96},{96,128},{128,160},{160,192},{192,224},{224... | collective-permute-start | bytes 1769480 | tf_op jit(solution)/shard_map/ppermute | solution.py:31
  366.2 66.3 %collective-permute-start.8 = (f32[2,768,384]{2,1,0:T(8,128)}, f32[2,768,384]{2,1,0:T(8,128)}, u32[]{:S(2)}, u32[]{:S(2)}) collective-permute-start(f32[2,768,384]{2,1,0:T(8,128)} %copy.399), channel_id=1, source_target_pairs={{0,1},{1,2},{2,3},{3,4},{4,5},{5,6},{6,7},{7,8},{8,9},{9,10},{10,1... | collective-permute-start | bytes 7077896 | tf_op jit(solution)/shard_map/ppermute | solution.py:16
  373.3 2.4 copy-start.23
  373.3 2.4 copy-start.24
  380.6 51.9 %collective-permute-start.7 = (f32[2,768,384]{2,1,0:T(8,128)}, f32[2,768,384]{2,1,0:T(8,128)}, u32[]{:S(2)}, u32[]{:S(2)}) collective-permute-start(f32[2,768,384]{2,1,0:T(8,128)} %copy.390), channel_id=1, source_target_pairs={{1,0},{2,1},{3,2},{4,3},{5,4},{6,5},{7,6},{8,7},{9,8},{10,9},{11,1... | collective-permute-start | bytes 7077896 | tf_op jit(solution)/shard_map/ppermute | solution.py:16
  393.3 1.4 copy-start.22
  396.1 1.7 copy-start.11
  401.6 4.9 %copy-start.10 = (bf16[2,768,384]{2,1,0:T(8,128)(2,1)S(1)}, bf16[2,768,384]{2,1,0:T(8,128)(2,1)}, u32[]{:S(2)}) copy-start(bf16[2,768,384]{2,1,0:T(8,128)(2,1)} %get-tuple-element.103) | copy-start | bytes 3538948
  410.3 3.9 copy-start.16
  411.8 3.7 copy-start.19
  414.2 2.5 copy-start.12
  415.5 2.5 copy-start.17
  416.7 2.5 copy-start.20
  418.0 3.7 copy-start.9
  436.8 1.3 copy-start.5
  436.8 1.6 copy-start.7
  436.9 3.2 copy-start.1
Sparse Core Ops, SparseCore 0:
  78.2 184.3 all-reduce.3
where the time goes:
time: 449 us; the launch traced here: 447 us
  waiting for transfers between devices  206 us (46%)
  local copies, waits for them, and re-layouts  126 us (28%)
  starting transfers between devices  45.9 us (10%)
  matrix products  31.2 us (7%)
  other arithmetic  24 us (5%)
  between operations  14.3 us (3%)
    psum x1, waiting for transfers between devices, broadcast(): return lax.psum(block, axis)  178 us
    unnamed x123, local copies, waits for them, and re-layouts  32.1 us
    ppermute x5, waiting for transfers between devices, passed_along(): return lax.ppermute(block, axis, route)  27.5 us
    ppermute x5, starting transfers between devices, passed_along(): return lax.ppermute(block, axis, route)  25.3 us
    another operation x12, local copies, waits for them, and re-layouts, column_windows(): jnp.stack([spread_field[:, :, q * BLK:q * BLK + width] for q in range(2 *...  24.4 us
    ppermute x2, starting transfers between devices, padded_2(): before = lax.ppermute(last, axis, up)  16.8 us
    another operation x6, local copies, waits for them, and re-layouts, band_blocks(): return jnp.stack(pieces, axis=1)  15 us
    dot_general x12, matrix products, rate(): jnp.einsum('piy,yx->pix', blocks[:, :, k], column_band[k, edge - k], pref...  10 us
  transfers between devices with their start and end apart: 10, of which 3 were waited for; matrix products, arithmetic and copies ran while one was open for 35% of the time, Pallas kernels for 0%

commit v1 on v0

v1 whole, which is shorter than its diff:
```python
import jax
import jax.numpy as jnp
from jax import lax
from jax.experimental import pallas as pl
from jax.experimental.pallas import tpu as pltpu
from jax.sharding import PartitionSpec as P

BLK = 128
BAND = 3
DT = 0.5

Y_HI, X, CORE = 2, 4, 2
Y_LO, Z = 4, 8
ROWS = Y_HI * X * CORE
COLS = Y_LO * Z
TALL = 6 * BLK
WIDE = 3 * BLK
MARGIN = BAND * BLK
PAIR = 2 * BLK
HALF = TALL // 2

CROSSING = [(r, p) for r in range(-BAND, 0) for p in range(1, BAND + 1) if r + p >= 0]

F32 = jnp.float32
BF16 = jnp.bfloat16
MIB = 1 << 20
VMEM = pl.BlockSpec(memory_space=pltpu.VMEM)


def params(mib):
    return pltpu.CompilerParams(vmem_limit_bytes=mib * MIB)


def cost(flops, bytes_accessed):
    return pl.CostEstimate(flops=flops, bytes_accessed=bytes_accessed, transcendentals=0)


def to_column(block, distance):
    return lax.ppermute(block, "col", [(i - distance, i) for i in range(COLS) if 0 <= i - distance < COLS])


OWN_CHIPS = [
    16267594, 12429704, 9998170, 9706963, 16353610, 16038288, 10063690, 9809793, 10538199, 10538654, 15231692,
    13466180, 10538143, 10615892, 13421191, 12103196, 16300816, 15773016, 12074762, 11571098, 4109616,
    12428080, 3343851, 3343851, 11616129, 9801617, 16324931, 9973579, 16095632, 16300368, 9707418, 9969498,
]
CROSSING_CHIPS = [
    13973960, 10067778, 16259411, 9805712, 14432586, 9015153, 13998530, 12934852, 12701521, 14736596, 15551557,
    14805588, 11325062, 10776220, 11030110, 2258165, 4142376, 11580912, 4107544, 11541971, 4109616, 13713217,
    9995755, 9969498, 5345193, 16258347, 15741866, 16259411, 9748368, 9805712, 9969498,
]


def routes(kind, chips):
    pairs = []
    for tile in range(ROWS):
        for col in range(COLS):
            y_lo, z = divmod(col, Z)
            away = (z - 2 * tile + 1 - kind) % Z
            target = 2 * tile + away // 2 + kind
            if away < 4 and target < COLS:
                chip = chips[2 * tile + away // 2] >> 3 * (away % 2 * Y_LO + y_lo) & 7
                pairs.append((tile * COLS + col, (chip * CORE + kind) * COLS + target))
    return pairs


def core_index():
    return lax.rem(lax.axis_index("row"), CORE)


def start_kernel(hcols, hvals, top, bottom, upper, own, crossing, to_chip, to_core):
    tile = lax.axis_index("row")
    z = lax.rem(lax.axis_index("col"), Z)
    for i in range(6):
        b = tile * 6 + i
        upper[4 * i] = hvals[i, 0]
        for p in range(1, BAND + 1):
            block = jnp.zeros((BLK, BLK), BF16)
            for s in range(1, p + 1):
                block = jnp.where(hcols[i, s] == b + p, hvals[i, s], block)
            upper[4 * i + p] = block
    away = lax.rem(z - 2 * tile + 1 + 2 * ROWS, Z)
    half = lax.rem(away // 2, 2)
    own[...] = upper[pl.ds(half * 12, 12)]
    away = lax.rem(z - 2 * tile + 2 * ROWS, Z)
    half = lax.rem(away // 2, 2)
    for k, (r, p) in enumerate(CROSSING):
        crossing[k] = upper[half * 12 + 4 * (r + 3) + p]

    def fill(above, below):
        for part in range(2):
            for k in range(3):
                rows = slice(k * BLK, (k + 1) * BLK)
                above[3 * part + k] = top[part, rows]
                below[3 * part + k] = bottom[part, rows]
        for k, (r, p) in enumerate(CROSSING):
            below[6 + k // 3, :, k % 3 * BLK : (k % 3 + 1) * BLK] = upper[4 * (r + 6) + p]

    core = core_index()

    @pl.when(core == 0)
    def _():
        fill(to_chip, to_core)

    @pl.when(core == 1)
    def _():
        fill(to_core, to_chip)


def both(block):
    wide = block.astype(F32)
    return (wide + wide.T).astype(BF16)


def right_band_kernel(halves, across, band):
    core = core_index()

    def own(k):
        return jnp.where(core == 0, halves[k], across[k])

    def crossing(k):
        return jnp.where(core == 0, across[k], halves[k])

    for r in range(9):
        for j in range(3):
            offset = j + BAND - r
            if abs(offset) > BAND:
                block = jnp.zeros((BLK, BLK), BF16)
            elif offset > 0 and r < BAND:
                block = crossing(CROSSING.index((r - BAND, offset)))
            elif offset > 0:
                block = own(4 * (r - BAND) + offset)
            elif offset == 0:
                block = both(own(4 * j))
            else:
                block = own(4 * j - offset).T
            band[r * BLK : (r + 1) * BLK, j * BLK : (j + 1) * BLK] = block


def left_products(band, ext, pair):
    return jnp.dot(band[pair], ext[pair * PAIR : pair * PAIR + 1024, :], preferred_element_type=F32)


def first_left_kernel(field, from_chip, from_core, upper, out, band, ext):
    core = core_index()
    for part in range(2):
        at = slice(part * WIDE, (part + 1) * WIDE)
        for k in range(3):
            one, two = from_chip[3 * part + k], from_core[3 * part + k]
            ext[k * BLK : (k + 1) * BLK, at] = jnp.where(core == 0, one, two)
            ext[MARGIN + TALL + k * BLK : MARGIN + TALL + (k + 1) * BLK, at] = jnp.where(core == 0, two, one)
        ext[MARGIN : MARGIN + TALL, at] = field[part]

    def low(k):
        at = slice(k % 3 * BLK, (k % 3 + 1) * BLK)
        return jnp.where(core == 0, from_chip[6 + k // 3, :, at], from_core[6 + k // 3, :, at])

    for pair in range(3):
        for i in range(2):
            b = 2 * pair + i
            for c in range(8):
                offset = c - BAND - i
                if abs(offset) > BAND:
                    block = jnp.zeros((BLK, BLK), BF16)
                elif offset > 0:
                    block = upper[4 * b + offset]
                elif offset == 0:
                    block = both(upper[4 * b])
                elif b + offset >= 0:
                    block = upper[4 * (b + offset) - offset].T
                else:
                    block = low(CROSSING.index((b + offset, -offset))).T
                band[pair, i * BLK : (i + 1) * BLK, c * BLK : (c + 1) * BLK] = block
    for pair in range(3):
        product = left_products(band, ext, pair)
        rows = slice(pair * PAIR, (pair + 1) * PAIR)
        out[0, rows] = product[:, :WIDE]
        out[1, rows] = product[:, WIDE:]


def first_right_kernel(before, field, after, other, left, band, middle, total, to_chip, to_core):
    stretch = jnp.concatenate([before[0], field[0], after[0]], axis=1)
    product = jnp.concatenate(
        [
            jnp.dot(stretch[:, :1024], band[:1024, :256], preferred_element_type=F32),
            jnp.dot(stretch[:, 256:], band[256:, 256:], preferred_element_type=F32),
        ],
        axis=1,
    )
    sign = jnp.where(pl.program_id(0) == 0, -1.0, 1.0)
    rate = sign * (left[0] - product)
    start = other[0].astype(F32)
    stepped = (start + DT * rate).astype(BF16)
    middle[0] = stepped
    total[0] = start + (DT / 2) * rate

    outward = pl.program_id(1) == core_index()

    @pl.when(outward)
    def _():
        to_chip[0] = stepped

    @pl.when(jnp.logical_not(outward))
    def _():
        to_core[0] = stepped


def second_left_kernel(middle, from_chip, from_core, band, right_band, total, out, ext):
    core = core_index()
    for part in range(2):
        at = slice(part * WIDE, (part + 1) * WIDE)
        one, two = from_chip[part], from_core[part]
        ext[:MARGIN, at] = jnp.where(core == 0, one, two)
        ext[MARGIN : MARGIN + TALL, at] = middle[part]
        ext[MARGIN + TALL :, at] = jnp.where(core == 0, two, one)
    centre = right_band[MARGIN : MARGIN + WIDE, :]
    for pair in range(3):
        rows = slice(pair * PAIR, (pair + 1) * PAIR)
        product = left_products(band, ext, pair)
        own_re = jnp.dot(middle[0, rows], centre, preferred_element_type=F32)
        own_im = jnp.dot(middle[1, rows], centre, preferred_element_type=F32)
        out[0, rows] = total[0, rows] + (DT / 2) * (product[:, WIDE:] - own_im)
        out[1, rows] = total[1, rows] - (DT / 2) * (product[:, :WIDE] - own_re)


def last_kernel(before, after, total, band, out):
    product = jnp.dot(before[0], band[:MARGIN, :], preferred_element_type=F32)
    product = product + jnp.dot(after[0], band[MARGIN + WIDE :, :], preferred_element_type=F32)
    sign = jnp.where(pl.program_id(0) == 0, 1.0, -1.0)
    out[0] = total[0] + (sign * DT / 2) * product


SAME = pl.BlockSpec((1, HALF, WIDE), lambda p, h: (p, h, 0))
OTHER = pl.BlockSpec((1, HALF, WIDE), lambda p, h: (1 - p, h, 0))
OTHER_EDGE = pl.BlockSpec((1, HALF, WIDE), lambda p, h: (1 - p, 0, 0))
BANDS = pl.BlockSpec((9 * BLK, WIDE), lambda p, h: (0, 0))


def to_other_core(block):
    return lax.ppermute(block, "row", [(i, i ^ 1) for i in range(ROWS)])


def to_other_chip(block):
    ends = [(i, i + 1) for i in range(1, ROWS - 1, 2)]
    return lax.ppermute(block, "row", ends + [(j, i) for i, j in ends])


def on_device(density, hcols, hvals):
    before = to_column(density, 1)
    after = to_column(density, -1)
    top = pl.BlockSpec((2, MARGIN, WIDE), lambda _: (0, 0, 0))
    bottom = pl.BlockSpec((2, MARGIN, WIDE), lambda _: (0, 1, 0))
    upper, own, crossing, to_chip, to_core = pl.pallas_call(
        start_kernel,
        grid=(1,),
        in_specs=[pl.BlockSpec(memory_space=pltpu.SMEM), VMEM, top, bottom],
        out_specs=[VMEM] * 5,
        out_shape=[
            jax.ShapeDtypeStruct((24, BLK, BLK), BF16),
            jax.ShapeDtypeStruct((12, BLK, BLK), BF16),
            jax.ShapeDtypeStruct((6, BLK, BLK), BF16),
            jax.ShapeDtypeStruct((8, BLK, WIDE), BF16),
            jax.ShapeDtypeStruct((8, BLK, WIDE), BF16),
        ],
        compiler_params=params(56),
        cost_estimate=cost(0, 4 * MIB),
        name="start",
    )(hcols, hvals, density, density)
    own = lax.ppermute(own, ("row", "col"), routes(0, OWN_CHIPS))
    crossing = lax.ppermute(crossing, ("row", "col"), routes(1, CROSSING_CHIPS))
    halves = jnp.where(core_index() == 0, own, jnp.concatenate([crossing, crossing], axis=0))
    across = to_other_core(halves)
    from_chip = to_other_chip(to_chip)
    from_core = to_other_core(to_core)
    left, left_band = pl.pallas_call(
        first_left_kernel,
        in_specs=[VMEM] * 4,
        out_specs=[VMEM] * 2,
        out_shape=[
            jax.ShapeDtypeStruct((2, TALL, WIDE), F32),
            jax.ShapeDtypeStruct((3, PAIR, 1024), BF16),
        ],
        scratch_shapes=[pltpu.VMEM((TALL + 2 * MARGIN, 2 * WIDE), BF16)],
        compiler_params=params(24),
        cost_estimate=cost(2 * TALL * 1024 * 2 * WIDE, 8 * MIB),
        name="first_left",
    )(density, from_chip, from_core, upper)
    right_band = pl.pallas_call(
        right_band_kernel,
        in_specs=[VMEM] * 2,
        out_specs=VMEM,
        out_shape=jax.ShapeDtypeStruct((9 * BLK, WIDE), BF16),
        compiler_params=params(16),
        cost_estimate=cost(0, 2 * MIB),
        name="right_band",
    )(halves, across)
    middle, total, to_chip, to_core = pl.pallas_call(
        first_right_kernel,
        grid=(2, 2),
        in_specs=[SAME, SAME, SAME, OTHER, SAME, BANDS],
        out_specs=[OTHER, OTHER, OTHER_EDGE, OTHER_EDGE],
        out_shape=[
            jax.ShapeDtypeStruct((2, TALL, WIDE), BF16),
            jax.ShapeDtypeStruct((2, TALL, WIDE), F32),
            jax.ShapeDtypeStruct((2, MARGIN, WIDE), BF16),
            jax.ShapeDtypeStruct((2, MARGIN, WIDE), BF16),
        ],
        compiler_params=params(24),
        cost_estimate=cost(4 * TALL * 9 * BLK * WIDE, 14 * MIB),
        name="first_right",
    )(before, density, after, density, left, right_band)

    before = to_column(middle, 1)
    after = to_column(middle, -1)
    from_chip = to_other_chip(to_chip)
    from_core = to_other_core(to_core)
    total = pl.pallas_call(
        second_left_kernel,
        in_specs=[VMEM] * 6,
        out_specs=VMEM,
        out_shape=jax.ShapeDtypeStruct((2, TALL, WIDE), F32),
        scratch_shapes=[pltpu.VMEM((TALL + 2 * MARGIN, 2 * WIDE), BF16)],
        compiler_params=params(32),
        cost_estimate=cost(2 * TALL * 1408 * 2 * WIDE, 10 * MIB),
        name="second_left",
    )(middle, from_chip, from_core, left_band, right_band, total)
    return pl.pallas_call(
        last_kernel,
        grid=(2, 2),
        in_specs=[SAME, SAME, OTHER, BANDS],
        out_specs=OTHER,
        out_shape=jax.ShapeDtypeStruct((2, TALL, WIDE), F32),
        compiler_params=params(24),
        cost_estimate=cost(4 * TALL * 6 * BLK * WIDE, 8 * MIB),
        name="last",
    )(before, after, total, right_band)


def solution(mesh):
    placed = (P(None, "row", "col"), P("row", None), P("row", None, None, None))
    return jax.shard_map(
        on_device, mesh=mesh, in_specs=placed, out_specs=P(None, "row", "col"), check_vma=False
    )
```

time: 449 us -> 117 us (0.26)
  waiting for transfers between devices: 206 us -> 60.4 us
  local copies, waits for them, and re-layouts: 126 us -> 1.36 us
  matrix products: 31.2 us -> 0 us
  other arithmetic: 24 us -> 1.07 us
  Pallas kernels: 0 us -> 14.5 us
  between operations: 14.3 us -> 0.18 us
  starting transfers between devices: 45.9 us -> 39.2 us
    psum x1 -> x0, waiting for transfers between devices: 178 us -> none  [broadcast(): return lax.psum(block, axis)]
    another operation x24 -> x0, local copies, waits for them, and re-layouts: 47.2 us -> none  [the longest x12 24.4 us: column_windows(): jnp.stack([spread_field[:, :, q * BLK:q * BLK + width] for q in range(2 *...]
    ppermute x9 -> x11, waiting for transfers between devices: 27.5 us -> 60.4 us  [the longest x2 45.4 us: to_other_chip(): return lax.ppermute(block, 'row', ends + [(j, i) for i, j in ends])]
    dot_general x29 -> x0, matrix products: 31.2 us -> none  [the longest x12 10 us: rate(): jnp.einsum('piy,yx->pix', blocks[:, :, k], column_band[k, edge - k], pref...]
    unnamed x123 -> x5, local copies, waits for them, and re-layouts: 32.1 us -> 1.36 us
    reshape x6 -> x0, local copies, waits for them, and re-layouts: 18.6 us -> none  [the longest x2 6.33 us: rate(): high_edge = jnp.stack(high_terms, axis=2).reshape(2, height, margin)]
    slice x12 -> x0, local copies, waits for them, and re-layouts: 17.8 us -> none  [the longest x5 9.24 us: column_windows(): spread_field[:, :, q * BLK:q * BLK + width]]
    pallas_call x0 -> x6, Pallas kernels: none -> 14.5 us  [the longest x1 3.46 us: on_device(): pl.pallas_call(start_kernel, grid=(1,), in_specs=[pl.BlockSpec(memory_spa...]
  transfers between devices with their start and end apart: 10 -> 11, of which waited for: 3 -> 5; matrix products, arithmetic and copies ran while one was open for 35% -> 2% of each run, Pallas kernels for 0% -> 7%
where the time goes in v1:
time: 117 us
  waiting for transfers between devices  60.4 us (52%)
  starting transfers between devices  39.2 us (34%)
  Pallas kernels  14.5 us (12%)
  local copies, waits for them, and re-layouts  1.36 us (1%)
    ppermute x2, waiting for transfers between devices, to_other_chip(): return lax.ppermute(block, 'row', ends + [(j, i) for i, j in ends])  45.4 us
    ppermute x4, starting transfers between devices, to_column(): lax.ppermute(block, 'col', [(i - distance, i) for i in range(COLS) if 0 <...  17.7 us
    ppermute x1, waiting for transfers between devices, on_device(): crossing = lax.ppermute(crossing, ('row', 'col'), routes(1, CROSSING_CHIPS))  10.8 us
    ppermute x1, starting transfers between devices, on_device(): own = lax.ppermute(own, ('row', 'col'), routes(0, OWN_CHIPS))  7.56 us
    ppermute x2, starting transfers between devices, to_other_chip(): return lax.ppermute(block, 'row', ends + [(j, i) for i, j in ends])  6.25 us
    ppermute x3, starting transfers between devices, to_other_core(): return lax.ppermute(block, 'row', [(i, i ^ 1) for i in range(ROWS)])  5.75 us
    pallas_call x1, Pallas kernels, on_device(): pl.pallas_call(start_kernel, grid=(1,), in_specs=[pl.BlockSpec(memory_spa...  3.46 us
    pallas_call x1, Pallas kernels, on_device(): pl.pallas_call(last_kernel, grid=(2, 2), in_specs=[SAME, SAME, OTHER, BAN...  3.2 us
  transfers between devices with their start and end apart: 11, of which 5 were waited for; matrix products, arithmetic and copies ran while one was open for 2% of the time, Pallas kernels for 7%

profile of v1, /device:TPU:15, one launch (start us, length us, event | category | flops | bytes accessed | tf_op | source)
XLA Modules:
  0.0 116.7 jit_solution(6562784358127533606)
XLA Ops:
  0.0 10.5 %collective-permute-start.1 = (bf16[2,768,384]{2,1,0:T(8,128)(2,1)}, bf16[2,768,384]{2,1,0:T(8,128)(2,1)S(1)}, u32[]{:S(2)}, u32[]{:S(2)}) collective-permute-start(bf16[2,768,384]{2,1,0:T(8,128)(2,1)} %other.1), channel_id=1, source_target_pairs={{1,0},{2,1},{3,2},{4,3},{5,4},{6,5},{7,6},{8,7},{9,8},{10,9},{11,1... | collective-permute-start | bytes 3538952 | tf_op jit(solution)/shard_map/ppermute | solution.py:39
  10.6 1.9 %collective-permute-start = (bf16[2,768,384]{2,1,0:T(8,128)(2,1)}, bf16[2,768,384]{2,1,0:T(8,128)(2,1)S(1)}, u32[]{:S(2)}, u32[]{:S(2)}) collective-permute-start(bf16[2,768,384]{2,1,0:T(8,128)(2,1)} %other.1), channel_id=1, source_target_pairs={{0,1},{1,2},{2,3},{3,4},{4,5},{5,6},{6,7},{7,8},{8,9},{9,10},{10,1... | collective-permute-start | bytes 3538952 | tf_op jit(solution)/shard_map/ppermute | solution.py:39
  12.5 1.3 %copy.4.hcols = s32[6,4]{1,0:T(8,128)} copy(s32[6,4]{0,1:T(4,128)} %param.4) | data formatting | bytes 192 | tf_op args[1]
  13.8 3.5 %start.1 = (bf16[24,128,128]{2,1,0:T(8,128)(2,1)}, bf16[12,128,128]{2,1,0:T(8,128)(2,1)}, bf16[6,128,128]{2,1,0:T(8,128)(2,1)}, bf16[8,128,384]{2,1,0:T(8,128)(2,1)}, bf16[8,128,384]{2,1,0:T(8,128)(2,1)}) custom-call(s32[6,4]{1,0:T(8,128)} %copy.4.hcols, bf16[6,4,128,128]{3,2,1,0:T(8,128)(2,1)} %hvals.1, bf16[2,768,384]{2,1,0:T(8,128)(2,1)} %other.1, ...), custom_call_target="tpu_custom_call" | custom-call | bytes 4194304 | tf_op jit(solution)/shard_map/start/pallas_call | solution.py:253
  17.3 7.6 %collective-permute-start.4 = (bf16[12,128,128]{2,1,0:T(8,128)(2,1)}, bf16[12,128,128]{2,1,0:T(8,128)(2,1)S(1)}, u32[]{:S(2)}, u32[]{:S(2)}) collective-permute-start(bf16[12,128,128]{2,1,0:T(8,128)(2,1)} %get-tuple-element.20), channel_id=1, source_target_pairs={{0,192},{1,1},{2,129},{7,128},{8,0},{9,65},{10,193},{15,64},{16,38... | collective-permute-start | bytes 1179656 | tf_op jit(solution)/shard_map/ppermute | solution.py:269
  24.9 1.9 %collective-permute-start.5 = (bf16[6,128,128]{2,1,0:T(8,128)(2,1)}, bf16[6,128,128]{2,1,0:T(8,128)(2,1)}, u32[]{:S(2)}, u32[]{:S(2)}) collective-permute-start(bf16[6,128,128]{2,1,0:T(8,128)(2,1)} %get-tuple-element.21), channel_id=1, source_target_pairs={{0,33},{1,225},{2,162},{3,98},{8,97},{9,161},{10,34},{11,226},{16,... | collective-permute-start | bytes 589832 | tf_op jit(solution)/shard_map/ppermute | solution.py:270
  26.8 3.7 %collective-permute-start.2 = (bf16[8,128,384]{2,1,0:T(8,128)(2,1)}, bf16[8,128,384]{2,1,0:T(8,128)(2,1)S(1)}, u32[]{:S(2)}, u32[]{:S(2)}) collective-permute-start(bf16[8,128,384]{2,1,0:T(8,128)(2,1)} %get-tuple-element.16), channel_id=1, source_target_pairs={{32,64},{96,128},{160,192},{224,256},{288,320},{352,384},{416,448}... | collective-permute-start | bytes 2359304 | tf_op jit(solution)/shard_map/ppermute | solution.py:245
  30.5 10.8 %collective-permute-done.5 = bf16[6,128,128]{2,1,0:T(8,128)(2,1)} collective-permute-done((bf16[6,128,128]{2,1,0:T(8,128)(2,1)}, bf16[6,128,128]{2,1,0:T(8,128)(2,1)}, u32[]{:S(2)}, u32[]{:S(2)}) %collective-permute-start.5) | collective-permute-done | bytes 196640 | tf_op jit(solution)/shard_map/ppermute | solution.py:270
  41.3 1.9 %collective-permute-start.3 = (bf16[8,128,384]{2,1,0:T(8,128)(2,1)}, bf16[8,128,384]{2,1,0:T(8,128)(2,1)}, u32[]{:S(2)}, u32[]{:S(2)}) collective-permute-start(bf16[8,128,384]{2,1,0:T(8,128)(2,1)} %get-tuple-element.17), channel_id=1, source_target_pairs={{0,32},{32,0},{64,96},{96,64},{128,160},{160,128},{192,224},{224,1... | collective-permute-start | bytes 2359304 | tf_op jit(solution)/shard_map/ppermute | solution.py:240
  43.2 0.0 copy-start
  43.3 0.0 copy-start.1
  43.3 2.5 %collective-permute-done.4 = bf16[12,128,128]{2,1,0:T(8,128)(2,1)S(1)} collective-permute-done((bf16[12,128,128]{2,1,0:T(8,128)(2,1)}, bf16[12,128,128]{2,1,0:T(8,128)(2,1)S(1)}, u32[]{:S(2)}, u32[]{:S(2)}) %collective-permute-start.4) | collective-permute-done | bytes 393248 | tf_op jit(solution)/shard_map/ppermute | solution.py:269
  45.8 1.1 maximum_select_fusion.halves
  46.9 1.9 %collective-permute-start.6 = (bf16[12,128,128]{2,1,0:T(8,128)(2,1)S(1)}, bf16[12,128,128]{2,1,0:T(8,128)(2,1)S(1)}, u32[]{:S(2)}, u32[]{:S(2)}) collective-permute-start(bf16[12,128,128]{2,1,0:T(8,128)(2,1)S(1)} %maximum_select_fusion.halves), channel_id=1, source_target_pairs={{0,32},{32,0},{64,96},{96,64},{128,160},{160,128},{192,224},{224,1... | collective-permute-start | bytes 1179656 | tf_op jit(solution)/shard_map/ppermute | solution.py:240
  48.8 1.7 %collective-permute-done.6.across = bf16[12,128,128]{2,1,0:T(8,128)(2,1)S(1)} collective-permute-done((bf16[12,128,128]{2,1,0:T(8,128)(2,1)S(1)}, bf16[12,128,128]{2,1,0:T(8,128)(2,1)S(1)}, u32[]{:S(2)}, u32[]{:S(2)}) %collective-permute-start.6) | collective-permute-done | bytes 393248 | tf_op jit(solution)/shard_map/ppermute | solution.py:240
  50.5 0.2 right_band.1.band
  50.7 13.3 %collective-permute-done.2.from_chip = bf16[8,128,384]{2,1,0:T(8,128)(2,1)S(1)} collective-permute-done((bf16[8,128,384]{2,1,0:T(8,128)(2,1)}, bf16[8,128,384]{2,1,0:T(8,128)(2,1)S(1)}, u32[]{:S(2)}, u32[]{:S(2)}) %collective-permute-start.2) | collective-permute-done | bytes 786464 | tf_op jit(solution)/shard_map/ppermute | solution.py:245
  64.0 0.0 collective-permute-done.3.from_core
  64.0 0.0 copy-done
  64.0 0.0 copy-done.1
  64.0 2.7 %first_left.1 = (f32[2,768,384]{2,1,0:T(8,128)S(1)}, bf16[3,256,1024]{2,1,0:T(8,128)(2,1)S(1)}) custom-call(bf16[2,768,384]{2,1,0:T(8,128)(2,1)S(1)} %copy-done, bf16[8,128,384]{2,1,0:T(8,128)(2,1)S(1)} %collective-permute-done.2.from_chip, bf16[8,128,384]{2,1,0:T(8,128)(2,1)} %collective-permute-done.3.from_core, bf16[24,128,128]{2,1,0:T(8,128)(2,1)S(1)} %copy-done.1), custom_call_target="tpu_custom_call" | custom-call | flops 1207959552 | bytes 8388608 | tf_op jit(solution)/shard_map/first_left/pallas_call | solution.py:275
  66.7 0.0 collective-permute-done.1.after
  66.7 0.0 collective-permute-done.before
  66.7 2.7 %first_right.1 = (bf16[2,768,384]{2,1,0:T(8,128)(2,1)S(1)}, f32[2,768,384]{2,1,0:T(8,128)S(1)}, bf16[2,384,384]{2,1,0:T(8,128)(2,1)S(1)}, bf16[2,384,384]{2,1,0:T(8,128)(2,1)S(1)}) custom-call(bf16[2,768,384]{2,1,0:T(8,128)(2,1)S(1)} %collective-permute-done.before, bf16[2,768,384]{2,1,0:T(8,128)(2,1)S(1)} %copy-done, ...), custom_call_target="tpu_custom_call" | custom-call | flops 1358954496 | bytes 14680064 | tf_op jit(solution)/shard_map/first_right/pallas_call | solution.py:297
  69.4 1.9 %collective-permute-start.8 = (bf16[2,768,384]{2,1,0:T(8,128)(2,1)S(1)}, bf16[2,768,384]{2,1,0:T(8,128)(2,1)S(1)}, u32[]{:S(2)}, u32[]{:S(2)}) collective-permute-start(bf16[2,768,384]{2,1,0:T(8,128)(2,1)S(1)} %get-tuple-element.22.middle), channel_id=1, source_target_pairs={{1,0},{2,1},{3,2},{4,3},{5,4},{6,5},{7,6},{8,7},{9,8},{10,9},{11,1... | collective-permute-start | bytes 3538952 | tf_op jit(solution)/shard_map/ppermute | solution.py:39
  71.3 3.4 %collective-permute-start.7 = (bf16[2,768,384]{2,1,0:T(8,128)(2,1)S(1)}, bf16[2,768,384]{2,1,0:T(8,128)(2,1)S(1)}, u32[]{:S(2)}, u32[]{:S(2)}) collective-permute-start(bf16[2,768,384]{2,1,0:T(8,128)(2,1)S(1)} %get-tuple-element.22.middle), channel_id=1, source_target_pairs={{0,1},{1,2},{2,3},{3,4},{4,5},{5,6},{6,7},{7,8},{8,9},{9,10},{10,1... | collective-permute-start | bytes 3538952 | tf_op jit(solution)/shard_map/ppermute | solution.py:39
  74.7 2.5 %collective-permute-start.9 = (bf16[2,384,384]{2,1,0:T(8,128)(2,1)S(1)}, bf16[2,384,384]{2,1,0:T(8,128)(2,1)S(1)}, u32[]{:S(2)}, u32[]{:S(2)}) collective-permute-start(bf16[2,384,384]{2,1,0:T(8,128)(2,1)S(1)} %get-tuple-element.23), channel_id=1, source_target_pairs={{32,64},{96,128},{160,192},{224,256},{288,320},{352,384},{416,448}... | collective-permute-start | bytes 1769480 | tf_op jit(solution)/shard_map/ppermute | solution.py:245
  77.2 1.9 %collective-permute-start.10 = (bf16[2,384,384]{2,1,0:T(8,128)(2,1)S(1)}, bf16[2,384,384]{2,1,0:T(8,128)(2,1)S(1)}, u32[]{:S(2)}, u32[]{:S(2)}) collective-permute-start(bf16[2,384,384]{2,1,0:T(8,128)(2,1)S(1)} %get-tuple-element.24), channel_id=1, source_target_pairs={{0,32},{32,0},{64,96},{96,64},{128,160},{160,128},{192,224},{224,1... | collective-permute-start | bytes 1769480 | tf_op jit(solution)/shard_map/ppermute | solution.py:240
  79.1 32.2 %collective-permute-done.9.from_chip = bf16[2,384,384]{2,1,0:T(8,128)(2,1)S(1)} collective-permute-done((bf16[2,384,384]{2,1,0:T(8,128)(2,1)S(1)}, bf16[2,384,384]{2,1,0:T(8,128)(2,1)S(1)}, u32[]{:S(2)}, u32[]{:S(2)}) %collective-permute-start.9) | collective-permute-done | bytes 589856 | tf_op jit(solution)/shard_map/ppermute | solution.py:245
  111.3 0.0 collective-permute-done.10.from_core
  111.3 2.2 %second_left.1.total = f32[2,768,384]{2,1,0:T(8,128)S(1)} custom-call(bf16[2,768,384]{2,1,0:T(8,128)(2,1)S(1)} %get-tuple-element.22.middle, bf16[2,384,384]{2,1,0:T(8,128)(2,1)S(1)} %collective-permute-done.9.from_chip, bf16[2,384,384]{2,1,0:T(8,128)(2,1)S(1)} %collective-permute-done.10.from_core, bf16[3,256,1024]{2,1,0:T(8,128)(2,1)S(1)} %get-tuple-element.25.band, ...), custom_call_target="tpu_custom_call" | custom-call | flops 1660944384 | bytes 10485760 | tf_op jit(solution)/shard_map/second_left/pallas_call | solution.py:317
  113.5 0.0 collective-permute-done.8.after
  113.5 0.0 collective-permute-done.7.before
  113.5 3.2 %last.1 = f32[2,768,384]{2,1,0:T(8,128)} custom-call(bf16[2,768,384]{2,1,0:T(8,128)(2,1)S(1)} %collective-permute-done.7.before, bf16[2,768,384]{2,1,0:T(8,128)(2,1)S(1)} %collective-permute-done.8.after, f32[2,768,384]{2,1,0:T(8,128)S(1)} %second_left.1.total, bf16[1152,384]{1,0:T(8,128)(2,1)S(1)} %right_band.1.band), custom_call_target="tpu_custom_call" | custom-call | flops 905969664 | bytes 8388608 | tf_op jit(solution)/shard_map/last/pallas_call | solution.py:327
Async XLA Ops:
  0.0 66.7 %collective-permute-start.1 = (bf16[2,768,384]{2,1,0:T(8,128)(2,1)}, bf16[2,768,384]{2,1,0:T(8,128)(2,1)S(1)}, u32[]{:S(2)}, u32[]{:S(2)}) collective-permute-start(bf16[2,768,384]{2,1,0:T(8,128)(2,1)} %other.1), channel_id=1, source_target_pairs={{1,0},{2,1},{3,2},{4,3},{5,4},{6,5},{7,6},{8,7},{9,8},{10,9},{11,1... | collective-permute-start | bytes 3538952 | tf_op jit(solution)/shard_map/ppermute | solution.py:39
  10.6 56.1 %collective-permute-start = (bf16[2,768,384]{2,1,0:T(8,128)(2,1)}, bf16[2,768,384]{2,1,0:T(8,128)(2,1)S(1)}, u32[]{:S(2)}, u32[]{:S(2)}) collective-permute-start(bf16[2,768,384]{2,1,0:T(8,128)(2,1)} %other.1), channel_id=1, source_target_pairs={{0,1},{1,2},{2,3},{3,4},{4,5},{5,6},{6,7},{7,8},{8,9},{9,10},{10,1... | collective-permute-start | bytes 3538952 | tf_op jit(solution)/shard_map/ppermute | solution.py:39
  17.3 28.5 %collective-permute-start.4 = (bf16[12,128,128]{2,1,0:T(8,128)(2,1)}, bf16[12,128,128]{2,1,0:T(8,128)(2,1)S(1)}, u32[]{:S(2)}, u32[]{:S(2)}) collective-permute-start(bf16[12,128,128]{2,1,0:T(8,128)(2,1)} %get-tuple-element.20), channel_id=1, source_target_pairs={{0,192},{1,1},{2,129},{7,128},{8,0},{9,65},{10,193},{15,64},{16,38... | collective-permute-start | bytes 1179656 | tf_op jit(solution)/shard_map/ppermute | solution.py:269
  24.9 16.5 %collective-permute-start.5 = (bf16[6,128,128]{2,1,0:T(8,128)(2,1)}, bf16[6,128,128]{2,1,0:T(8,128)(2,1)}, u32[]{:S(2)}, u32[]{:S(2)}) collective-permute-start(bf16[6,128,128]{2,1,0:T(8,128)(2,1)} %get-tuple-element.21), channel_id=1, source_target_pairs={{0,33},{1,225},{2,162},{3,98},{8,97},{9,161},{10,34},{11,226},{16,... | collective-permute-start | bytes 589832 | tf_op jit(solution)/shard_map/ppermute | solution.py:270
  26.8 37.2 %collective-permute-start.2 = (bf16[8,128,384]{2,1,0:T(8,128)(2,1)}, bf16[8,128,384]{2,1,0:T(8,128)(2,1)S(1)}, u32[]{:S(2)}, u32[]{:S(2)}) collective-permute-start(bf16[8,128,384]{2,1,0:T(8,128)(2,1)} %get-tuple-element.16), channel_id=1, source_target_pairs={{32,64},{96,128},{160,192},{224,256},{288,320},{352,384},{416,448}... | collective-permute-start | bytes 2359304 | tf_op jit(solution)/shard_map/ppermute | solution.py:245
  41.3 22.7 %collective-permute-start.3 = (bf16[8,128,384]{2,1,0:T(8,128)(2,1)}, bf16[8,128,384]{2,1,0:T(8,128)(2,1)}, u32[]{:S(2)}, u32[]{:S(2)}) collective-permute-start(bf16[8,128,384]{2,1,0:T(8,128)(2,1)} %get-tuple-element.17), channel_id=1, source_target_pairs={{0,32},{32,0},{64,96},{96,64},{128,160},{160,128},{192,224},{224,1... | collective-permute-start | bytes 2359304 | tf_op jit(solution)/shard_map/ppermute | solution.py:240
  43.2 20.8 %copy-start = (bf16[2,768,384]{2,1,0:T(8,128)(2,1)S(1)}, bf16[2,768,384]{2,1,0:T(8,128)(2,1)}, u32[]{:S(2)}) copy-start(bf16[2,768,384]{2,1,0:T(8,128)(2,1)} %other.1) | copy-start | bytes 3538948
  43.3 20.7 %copy-start.1 = (bf16[24,128,128]{2,1,0:T(8,128)(2,1)S(1)}, bf16[24,128,128]{2,1,0:T(8,128)(2,1)}, u32[]{:S(2)}) copy-start(bf16[24,128,128]{2,1,0:T(8,128)(2,1)} %get-tuple-element.18.upper) | copy-start | bytes 2359300
  46.9 3.6 %collective-permute-start.6 = (bf16[12,128,128]{2,1,0:T(8,128)(2,1)S(1)}, bf16[12,128,128]{2,1,0:T(8,128)(2,1)S(1)}, u32[]{:S(2)}, u32[]{:S(2)}) collective-permute-start(bf16[12,128,128]{2,1,0:T(8,128)(2,1)S(1)} %maximum_select_fusion.halves), channel_id=1, source_target_pairs={{0,32},{32,0},{64,96},{96,64},{128,160},{160,128},{192,224},{224,1... | collective-permute-start | bytes 1179656 | tf_op jit(solution)/shard_map/ppermute | solution.py:240
  69.4 44.1 %collective-permute-start.8 = (bf16[2,768,384]{2,1,0:T(8,128)(2,1)S(1)}, bf16[2,768,384]{2,1,0:T(8,128)(2,1)S(1)}, u32[]{:S(2)}, u32[]{:S(2)}) collective-permute-start(bf16[2,768,384]{2,1,0:T(8,128)(2,1)S(1)} %get-tuple-element.22.middle), channel_id=1, source_target_pairs={{1,0},{2,1},{3,2},{4,3},{5,4},{6,5},{7,6},{8,7},{9,8},{10,9},{11,1... | collective-permute-start | bytes 3538952 | tf_op jit(solution)/shard_map/ppermute | solution.py:39
  71.3 42.2 %collective-permute-start.7 = (bf16[2,768,384]{2,1,0:T(8,128)(2,1)S(1)}, bf16[2,768,384]{2,1,0:T(8,128)(2,1)S(1)}, u32[]{:S(2)}, u32[]{:S(2)}) collective-permute-start(bf16[2,768,384]{2,1,0:T(8,128)(2,1)S(1)} %get-tuple-element.22.middle), channel_id=1, source_target_pairs={{0,1},{1,2},{2,3},{3,4},{4,5},{5,6},{6,7},{7,8},{8,9},{9,10},{10,1... | collective-permute-start | bytes 3538952 | tf_op jit(solution)/shard_map/ppermute | solution.py:39
  74.7 36.6 %collective-permute-start.9 = (bf16[2,384,384]{2,1,0:T(8,128)(2,1)S(1)}, bf16[2,384,384]{2,1,0:T(8,128)(2,1)S(1)}, u32[]{:S(2)}, u32[]{:S(2)}) collective-permute-start(bf16[2,384,384]{2,1,0:T(8,128)(2,1)S(1)} %get-tuple-element.23), channel_id=1, source_target_pairs={{32,64},{96,128},{160,192},{224,256},{288,320},{352,384},{416,448}... | collective-permute-start | bytes 1769480 | tf_op jit(solution)/shard_map/ppermute | solution.py:245
  77.2 34.1 %collective-permute-start.10 = (bf16[2,384,384]{2,1,0:T(8,128)(2,1)S(1)}, bf16[2,384,384]{2,1,0:T(8,128)(2,1)S(1)}, u32[]{:S(2)}, u32[]{:S(2)}) collective-permute-start(bf16[2,384,384]{2,1,0:T(8,128)(2,1)S(1)} %get-tuple-element.24), channel_id=1, source_target_pairs={{0,32},{32,0},{64,96},{96,64},{128,160},{160,128},{192,224},{224,1... | collective-permute-start | bytes 1769480 | tf_op jit(solution)/shard_map/ppermute | solution.py:240

commit v2 on v1

v2 whole, which is shorter than its diff:
```python
import functools

import jax
import jax.numpy as jnp
from jax import lax
from jax.experimental import pallas as pl
from jax.experimental.pallas import tpu as pltpu
from jax.sharding import PartitionSpec as P

BLK = 128
BAND = 3
DT = 0.5

Y_HI, X, CORE = 2, 4, 2
Y_LO, Z = 4, 8
ROWS = Y_HI * X * CORE
COLS = Y_LO * Z
TALL = 6 * BLK
WIDE = 3 * BLK
MARGIN = BAND * BLK
PAIR = 2 * BLK
HALF = TALL // 2

CROSSING = [(r, p) for r in range(-BAND, 0) for p in range(1, BAND + 1) if r + p >= 0]

F32 = jnp.float32
BF16 = jnp.bfloat16
MIB = 1 << 20
VMEM = pl.BlockSpec(memory_space=pltpu.VMEM)


def params(mib):
    return pltpu.CompilerParams(vmem_limit_bytes=mib * MIB)


def cost(flops, bytes_accessed):
    return pl.CostEstimate(flops=flops, bytes_accessed=bytes_accessed, transcendentals=0)


def to_column(block, distance):
    return lax.ppermute(block, "col", [(i - distance, i) for i in range(COLS) if 0 <= i - distance < COLS])


OWN_CHIPS = [
    0o57234610, 0o65324710, 0o47106532, 0o46217530, 0o75104623, 0o65314720, 0o47205631, 0o46107523, 0o41356207,
    0o61354207, 0o72046135, 0o42067135, 0o71354206, 0o41357206, 0o72064135, 0o76024135, 0o37516402, 0o17502463,
    0o24631750, 0o14602753, 0o37521460, 0o7632451, 0o14523760, 0o2735461, 0o64027513, 0o54217603, 0o76035421,
    0o75206413, 0o46137520, 0o75234601, 0o76015423, 0o65137420,
]
CROSSING_CHIPS = [
    0o46207531, 0o45107623, 0o67124530, 0o45126730, 0o65104732, 0o47325610, 0o57304612, 0o71045236, 0o50264731,
    0o60145732, 0o57324016, 0o62345017, 0o50176324, 0o72165034, 0o50246713, 0o23645017, 0o34721560, 0o54723601,
    0o36510472, 0o14520673, 0o56732401, 0o46032571, 0o17532640, 0o75136402, 0o45107623, 0o76034512, 0o46017523,
    0o76235401, 0o75106423, 0o56017423, 0o76235410,
]


def routes(kind, chips):
    pairs = []
    for tile in range(ROWS):
        for col in range(COLS):
            y_lo, z = divmod(col, Z)
            away = (z - 2 * tile + 1 - kind) % Z
            target = 2 * tile + away // 2 + kind
            if away < 4 and target < COLS:
                chip = chips[2 * tile + away // 2] >> 3 * (away % 2 * Y_LO + y_lo) & 7
                pairs.append((tile * COLS + col, (chip * CORE + kind) * COLS + target))
    return pairs


def core_index():
    return lax.rem(lax.axis_index("row"), CORE)


def start_kernel(hcols, hvals, upper, own, crossing, low):
    tile = lax.axis_index("row")
    z = lax.rem(lax.axis_index("col"), Z)
    for i in range(6):
        b = tile * 6 + i
        upper[4 * i] = hvals[i, 0]
        for p in range(1, BAND + 1):
            block = jnp.zeros((BLK, BLK), BF16)
            for s in range(1, p + 1):
                named = jnp.broadcast_to(hcols[s : s + 1, i : i + 1] == b + p, (BLK, BLK))
                block = jnp.where(named, hvals[i, s], block)
            upper[4 * i + p] = block
    away = lax.rem(z - 2 * tile + 1 + 2 * ROWS, Z)
    half = lax.rem(away // 2, 2)
    own[...] = upper[pl.ds(half * 12, 12)]
    away = lax.rem(z - 2 * tile + 2 * ROWS, Z)
    half = lax.rem(away // 2, 2)
    for k, (r, p) in enumerate(CROSSING):
        crossing[k] = upper[half * 12 + 4 * (r + 3) + p]
        low[k // 3 * BLK : (k // 3 + 1) * BLK, k % 3 * BLK : (k % 3 + 1) * BLK] = upper[4 * (r + 6) + p]


def edge(density, low, row):
    rows = lax.dynamic_slice_in_dim(density, row, MARGIN, 1)
    return jnp.concatenate([rows.reshape(2 * MARGIN, WIDE), low], axis=0)


def both(block):
    wide = block.astype(F32)
    return (wide + wide.T).astype(BF16)


def right_band_kernel(halves, across, band):
    core = core_index()

    def own(k):
        return jnp.where(core == 0, halves[k], across[k])

    def crossing(k):
        return jnp.where(core == 0, across[k], halves[k])

    for r in range(9):
        for j in range(3):
            offset = j + BAND - r
            if abs(offset) > BAND:
                block = jnp.zeros((BLK, BLK), BF16)
            elif offset > 0 and r < BAND:
                block = crossing(CROSSING.index((r - BAND, offset)))
            elif offset > 0:
                block = own(4 * (r - BAND) + offset)
            elif offset == 0:
                block = both(own(4 * j))
            else:
                block = own(4 * j - offset).T
            band[r * BLK : (r + 1) * BLK, j * BLK : (j + 1) * BLK] = block


def inner_products(band, field, pair):
    first, stop = max(0, pair * PAIR - MARGIN), min(TALL, pair * PAIR + PAIR + MARGIN)
    columns = slice(first - pair * PAIR + MARGIN, stop - pair * PAIR + MARGIN)
    both_parts = jnp.concatenate([field[0, first:stop], field[1, first:stop]], axis=1)
    return jnp.dot(band[pair][:, columns], both_parts, preferred_element_type=F32)


def first_left_kernel(field, upper, out, band, below_band):
    for pair in range(3):
        for i in range(2):
            b = 2 * pair + i
            for c in range(8):
                offset = c - BAND - i
                if abs(offset) > BAND or b + offset < 0:
                    block = jnp.zeros((BLK, BLK), BF16)
                elif offset > 0:
                    block = upper[4 * b + offset]
                elif offset == 0:
                    block = both(upper[4 * b])
                else:
                    block = upper[4 * (b + offset) - offset].T
                band[pair, i * BLK : (i + 1) * BLK, c * BLK : (c + 1) * BLK] = block
    for i in range(3):
        for c in range(3):
            block = upper[4 * (3 + i) + 3 + c - i] if c <= i else jnp.zeros((BLK, BLK), BF16)
            below_band[i * BLK : (i + 1) * BLK, c * BLK : (c + 1) * BLK] = block
    for pair in range(3):
        product = inner_products(band, field, pair)
        rows = slice(pair * PAIR, (pair + 1) * PAIR)
        out[0, rows] = product[:, :WIDE]
        out[1, rows] = product[:, WIDE:]


def first_right_kernel(
    before, field, after, left, band, chip_far, core_far, below_band,
    middle, total, to_chip, to_core, above_band, from_chip, from_core, sems,
):
    core = core_index()
    copies = [
        pltpu.make_async_copy(far, near, sems.at[k])
        for k, (far, near) in enumerate(((chip_far, from_chip), (core_far, from_core)))
    ]
    for copy in copies:
        copy.start()
    for part in range(2):
        for k in range(2):
            rows = slice(k * MARGIN, (k + 1) * MARGIN)
            stretch = jnp.concatenate([before[part, rows], field[part, rows], after[part, rows]], axis=1)
            product = jnp.concatenate(
                [
                    jnp.dot(stretch[:, :1024], band[:1024, :256], preferred_element_type=F32),
                    jnp.dot(stretch[:, 256:], band[256:, 256:], preferred_element_type=F32),
                ],
                axis=1,
            )
            total[1 - part, rows] = left[part, rows] - product
    for copy in copies:
        copy.wait()
    for i in range(3):
        for c in range(3):
            block = jnp.zeros((BLK, BLK), BF16)
            if c >= i:
                k = CROSSING.index((c - 3, i + 3 - c))
                rows = slice(2 * MARGIN + k // 3 * BLK, 2 * MARGIN + (k // 3 + 1) * BLK)
                at = slice(k % 3 * BLK, (k % 3 + 1) * BLK)
                block = jnp.where(core == 0, from_chip[rows, at], from_core[rows, at]).T
            above_band[i * BLK : (i + 1) * BLK, c * BLK : (c + 1) * BLK] = block
    for part in range(2):
        other, sign = 1 - part, (-1.0, 1.0)[part]
        one, two = (side[part * MARGIN : (part + 1) * MARGIN] for side in (from_chip, from_core))
        halves = (
            (above_band, jnp.where(core == 0, one, two)),
            (below_band, jnp.where(core == 0, two, one)),
        )
        for k, (outer, beyond) in enumerate(halves):
            rows = slice(k * MARGIN, (k + 1) * MARGIN)
            far = jnp.dot(outer[...], beyond, preferred_element_type=F32)
            rate = sign * (total[other, rows] + far)
            start = field[other, rows].astype(F32)
            middle[other, rows] = (start + DT * rate).astype(BF16)
            total[other, rows] = start + (DT / 2) * rate
        to_chip[other] = middle[other, pl.ds(pl.multiple_of(core * MARGIN, MARGIN), MARGIN)]
        to_core[other] = middle[other, pl.ds(pl.multiple_of((1 - core) * MARGIN, MARGIN), MARGIN)]


def second_left_kernel(middle, band, right_band, total, out):
    centre = right_band[MARGIN : MARGIN + WIDE, :]
    for pair in range(3):
        rows = slice(pair * PAIR, (pair + 1) * PAIR)
        product = inner_products(band, middle, pair)
        own_re = jnp.dot(middle[0, rows], centre, preferred_element_type=F32)
        own_im = jnp.dot(middle[1, rows], centre, preferred_element_type=F32)
        out[0, rows] = total[0, rows] + (DT / 2) * (product[:, WIDE:] - own_im)
        out[1, rows] = total[1, rows] - (DT / 2) * (product[:, :WIDE] - own_re)


def last_kernel(before, after, total, band, from_chip, from_core, above_band, below_band, out, result, sems):
    core = core_index()
    copies = []
    for part in range(2):
        other, sign = 1 - part, (-1.0, 1.0)[part]
        halves = (
            (above_band, jnp.where(core == 0, from_chip[part], from_core[part])),
            (below_band, jnp.where(core == 0, from_core[part], from_chip[part])),
        )
        for k, (outer, beyond) in enumerate(halves):
            rows = slice(k * MARGIN, (k + 1) * MARGIN)
            product = jnp.dot(before[part, rows], band[:MARGIN, :], preferred_element_type=F32)
            product = product + jnp.dot(after[part, rows], band[MARGIN + WIDE :, :], preferred_element_type=F32)
            far = jnp.dot(outer[...], beyond, preferred_element_type=F32)
            result[other, rows] = total[other, rows] + (sign * DT / 2) * (far - product)
            at = pl.ds(k * MARGIN, MARGIN)
            copies.append(pltpu.make_async_copy(result.at[other, at], out.at[other, at], sems.at[2 * part + k]))
            copies[-1].start()
    for copy in copies:
        copy.wait()


def to_other_core(block):
    return lax.ppermute(block, "row", [(i, i ^ 1) for i in range(ROWS)])


def to_other_chip(block):
    ends = [(i, i + 1) for i in range(1, ROWS - 1, 2)]
    return lax.ppermute(block, "row", ends + [(j, i) for i, j in ends])


def on_device(density, hcols, hvals):
    before = to_column(density, 1)
    after = to_column(density, -1)
    any_space = pl.BlockSpec(memory_space=pl.ANY)
    upper, own, crossing, low = pl.pallas_call(
        start_kernel,
        in_specs=[VMEM] * 2,
        out_specs=[VMEM] * 4,
        out_shape=[
            jax.ShapeDtypeStruct((24, BLK, BLK), BF16),
            jax.ShapeDtypeStruct((12, BLK, BLK), BF16),
            jax.ShapeDtypeStruct((6, BLK, BLK), BF16),
            jax.ShapeDtypeStruct((2 * BLK, WIDE), BF16),
        ],
        compiler_params=params(56),
        cost_estimate=cost(0, 2 * MIB),
        name="start",
    )(hcols.T, hvals)
    to_chip = edge(density, low, core_index() * MARGIN)
    to_core = edge(density, low, (1 - core_index()) * MARGIN)
    own = lax.ppermute(own, ("row", "col"), routes(0, OWN_CHIPS))
    crossing = lax.ppermute(crossing, ("row", "col"), routes(1, CROSSING_CHIPS))
    left, left_band, below_band = pl.pallas_call(
        first_left_kernel,
        in_specs=[VMEM] * 2,
        out_specs=[VMEM] * 3,
        out_shape=[
            jax.ShapeDtypeStruct((2, TALL, WIDE), F32),
            jax.ShapeDtypeStruct((3, PAIR, 1024), BF16),
            jax.ShapeDtypeStruct((MARGIN, MARGIN), BF16),
        ],
        compiler_params=params(20),
        cost_estimate=cost(2 * TALL * 1024 * 2 * WIDE, 8 * MIB),
        name="first_left",
    )(density, upper)
    own, _ = lax.optimization_barrier((own, left_band))
    halves = jnp.where(core_index() == 0, own, jnp.concatenate([crossing, crossing], axis=0))
    across = to_other_core(halves)
    to_core, _ = lax.optimization_barrier((to_core, crossing))
    from_chip = to_other_chip(to_chip)
    from_core = to_other_core(to_core)
    right_band = pl.pallas_call(
        right_band_kernel,
        in_specs=[VMEM] * 2,
        out_specs=VMEM,
        out_shape=jax.ShapeDtypeStruct((9 * BLK, WIDE), BF16),
        compiler_params=params(16),
        cost_estimate=cost(0, 2 * MIB),
        name="right_band",
    )(halves, across)
    middle, total, to_chip, to_core, above_band = pl.pallas_call(
        first_right_kernel,
        in_specs=[VMEM] * 5 + [any_space] * 2 + [VMEM],
        out_specs=[VMEM] * 5,
        out_shape=[
            jax.ShapeDtypeStruct((2, TALL, WIDE), BF16),
            jax.ShapeDtypeStruct((2, TALL, WIDE), F32),
            jax.ShapeDtypeStruct((2, MARGIN, WIDE), BF16),
            jax.ShapeDtypeStruct((2, MARGIN, WIDE), BF16),
            jax.ShapeDtypeStruct((MARGIN, MARGIN), BF16),
        ],
        scratch_shapes=[pltpu.VMEM((2 * MARGIN + 2 * BLK, WIDE), BF16)] * 2 + [pltpu.SemaphoreType.DMA((2,))],
        compiler_params=params(20),
        cost_estimate=cost(4 * TALL * 9 * BLK * WIDE, 14 * MIB),
        name="first_right",
    )(before, density, after, left, right_band, from_chip, from_core, below_band)

    before = to_column(middle, 1)
    after = to_column(middle, -1)
    from_chip = to_other_chip(to_chip)
    from_core = to_other_core(to_core)
    total = pl.pallas_call(
        second_left_kernel,
        in_specs=[VMEM] * 4,
        out_specs=VMEM,
        out_shape=jax.ShapeDtypeStruct((2, TALL, WIDE), F32),
        compiler_params=params(24),
        cost_estimate=cost(2 * TALL * 1408 * 2 * WIDE, 10 * MIB),
        name="second_left",
    )(middle, left_band, right_band, total)
    return pl.pallas_call(
        last_kernel,
        in_specs=[VMEM] * 8,
        out_specs=any_space,
        out_shape=jax.ShapeDtypeStruct((2, TALL, WIDE), F32),
        scratch_shapes=[pltpu.VMEM((2, TALL, WIDE), F32), pltpu.SemaphoreType.DMA((4,))],
        compiler_params=params(16),
        cost_estimate=cost(4 * TALL * 6 * BLK * WIDE, 8 * MIB),
        name="last",
    )(before, after, total, right_band, from_chip, from_core, above_band, below_band)


def solution(mesh):
    placed = (P(None, "row", "col"), P("row", None), P("row", None, None, None))
    return jax.shard_map(
        on_device, mesh=mesh, in_specs=placed, out_specs=P(None, "row", "col"), check_vma=False
    )
```

time: 117 us -> 107 us (0.915)
  the two profiles are of different devices: /device:TPU:15 before, /device:TPU:496 now
where the time goes in v2:
time: 107 us
  waiting for transfers between devices  50.2 us (47%)
  starting transfers between devices  37.9 us (35%)
  Pallas kernels  13.5 us (13%)
  local copies, waits for them, and re-layouts  2.55 us (2%)
  other arithmetic  2.51 us (2%)
    ppermute x2, waiting for transfers between devices, to_other_chip(): return lax.ppermute(block, 'row', ends + [(j, i) for i, j in ends])  38.7 us
    ppermute x4, starting transfers between devices, to_column(): lax.ppermute(block, 'col', [(i - distance, i) for i in range(COLS) if 0 <...  15.9 us
    ppermute x2, starting transfers between devices, to_other_chip(): return lax.ppermute(block, 'row', ends + [(j, i) for i, j in ends])  12.4 us
    ppermute x1, waiting for transfers between devices, on_device(): own = lax.ppermute(own, ('row', 'col'), routes(0, OWN_CHIPS))  9.79 us
    ppermute x3, starting transfers between devices, to_other_core(): return lax.ppermute(block, 'row', [(i, i ^ 1) for i in range(ROWS)])  5.76 us
    pallas_call x1, Pallas kernels, on_device(): pl.pallas_call(first_right_kernel, in_specs=[VMEM] * 5 + [any_space] * 2...  4.44 us
    pallas_call x1, Pallas kernels, on_device(): pl.pallas_call(last_kernel, in_specs=[VMEM] * 8, out_specs=any_space, out...  3.17 us
    pallas_call x1, Pallas kernels, on_device(): pl.pallas_call(start_kernel, in_specs=[VMEM] * 2, out_specs=[VMEM] * 4, o...  2.58 us
  transfers between devices with their start and end apart: 11, of which 4 were waited for; matrix products, arithmetic and copies ran while one was open for 4% of the time, Pallas kernels for 6%

profile of v2, /device:TPU:496, one launch (start us, length us, event | category | flops | bytes accessed | tf_op | source)
XLA Modules:
  0.0 106.8 jit_solution(5028155193332341493)
XLA Ops:
  0.0 2.5 %collective-permute-start.1 = (bf16[2,768,384]{2,1,0:T(8,128)(2,1)}, bf16[2,768,384]{2,1,0:T(8,128)(2,1)S(1)}, u32[]{:S(2)}, u32[]{:S(2)}) collective-permute-start(bf16[2,768,384]{2,1,0:T(8,128)(2,1)} %field.3), channel_id=1, source_target_pairs={{1,0},{2,1},{3,2},{4,3},{5,4},{6,5},{7,6},{8,7},{9,8},{10,9},{11,1... | collective-permute-start | bytes 3538952 | tf_op jit(solution)/shard_map/ppermute | solution.py:41
  2.5 5.5 %collective-permute-start = (bf16[2,768,384]{2,1,0:T(8,128)(2,1)}, bf16[2,768,384]{2,1,0:T(8,128)(2,1)S(1)}, u32[]{:S(2)}, u32[]{:S(2)}) collective-permute-start(bf16[2,768,384]{2,1,0:T(8,128)(2,1)} %field.3), channel_id=1, source_target_pairs={{0,1},{1,2},{2,3},{3,4},{4,5},{5,6},{6,7},{7,8},{8,9},{9,10},{10,1... | collective-permute-start | bytes 3538952 | tf_op jit(solution)/shard_map/ppermute | solution.py:41
  8.0 2.6 %start.1 = (bf16[24,128,128]{2,1,0:T(8,128)(2,1)}, bf16[12,128,128]{2,1,0:T(8,128)(2,1)}, bf16[6,128,128]{2,1,0:T(8,128)(2,1)}, bf16[256,384]{1,0:T(8,128)(2,1)}) custom-call(s32[4,6]{1,0:T(4,128)} %bitcast.5, bf16[6,4,128,128]{3,2,1,0:T(8,128)(2,1)} %hvals.1), custom_call_target="tpu_custom_call" | custom-call | bytes 2097152 | tf_op jit(solution)/shard_map/start/pallas_call | solution.py:263
  10.5 1.3 %collective-permute-start.3 = (bf16[6,128,128]{2,1,0:T(8,128)(2,1)}, bf16[6,128,128]{2,1,0:T(8,128)(2,1)}, u32[]{:S(2)}, u32[]{:S(2)}) collective-permute-start(bf16[6,128,128]{2,1,0:T(8,128)(2,1)} %get-tuple-element.24), channel_id=1, source_target_pairs={{0,97},{1,33},{2,226},{3,34},{8,225},{9,161},{10,162},{11,98},{16,... | collective-permute-start | bytes 589832 | tf_op jit(solution)/shard_map/ppermute | solution.py:280
  11.9 2.4 %collective-permute-start.2 = (bf16[12,128,128]{2,1,0:T(8,128)(2,1)}, bf16[12,128,128]{2,1,0:T(8,128)(2,1)}, u32[]{:S(2)}, u32[]{:S(2)}) collective-permute-start(bf16[12,128,128]{2,1,0:T(8,128)(2,1)} %get-tuple-element.21), channel_id=1, source_target_pairs={{0,192},{1,1},{2,129},{7,0},{8,128},{9,65},{10,193},{15,64},{16,44... | collective-permute-start | bytes 1179656 | tf_op jit(solution)/shard_map/ppermute | solution.py:279
  14.3 0.0 copy-start.2
  14.3 1.4 %constant_dynamic-slice_fusion = (bf16[2,384,384]{2,1,0:T(8,128)(2,1)S(1)}, bf16[2,384,384]{2,1,0:T(8,128)(2,1)S(1)}) fusion(bf16[2,768,384]{2,1,0:T(8,128)(2,1)} %field.3, s32[]{:T(128)S(6)} %select_n.17, s32[]{:T(128)S(6)} %select_n.16), kind=kLoop, calls=%fused_computation.3 | loop fusion | bytes 2359304 | tf_op jit(solution)/shard_map/dynamic_slice | solution.py:98
  15.7 0.0 copy-start
  15.7 0.0 copy-done.2
  15.8 1.3 %pad_maximum_fusion = (bf16[1024,384]{1,0:T(8,128)(2,1)}, bf16[1024,384]{1,0:T(8,128)(2,1)}) fusion(bf16[256,384]{1,0:T(8,128)(2,1)S(1)} %copy-done.2, bf16[768,384]{1,0:T(8,128)(2,1)S(1)} %bitcast.3, bf16[768,384]{1,0:T(8,128)(2,1)S(1)} %bitcast.4), kind=kLoop, calls=%fused_computation | loop fusion | flops 2752512 | bytes 2949120 | tf_op jit(solution)/shard_map/concatenate | solution.py:99
  17.1 7.8 %collective-permute-start.5 = (bf16[1024,384]{1,0:T(8,128)(2,1)}, bf16[1024,384]{1,0:T(8,128)(2,1)}, u32[]{:S(2)}, u32[]{:S(2)}) collective-permute-start(bf16[1024,384]{1,0:T(8,128)(2,1)} %get-tuple-element.36), channel_id=1, source_target_pairs={{32,64},{96,128},{160,192},{224,256},{288,320},{352,384},{416,448}... | collective-permute-start | bytes 2359304 | tf_op jit(solution)/shard_map/ppermute | solution.py:256
  24.9 0.0 collective-permute-done.3
  24.9 1.9 %collective-permute-start.6 = (bf16[1024,384]{1,0:T(8,128)(2,1)}, bf16[1024,384]{1,0:T(8,128)(2,1)}, u32[]{:S(2)}, u32[]{:S(2)}) collective-permute-start(bf16[1024,384]{1,0:T(8,128)(2,1)} %get-tuple-element.26), channel_id=1, source_target_pairs={{0,32},{32,0},{64,96},{96,64},{128,160},{160,128},{192,224},{224,1... | collective-permute-start | bytes 2359304 | tf_op jit(solution)/shard_map/ppermute | solution.py:251
  26.9 0.0 copy-done
  26.9 0.0 copy-start.1
  26.9 1.1 %copy-done.1 = bf16[24,128,128]{2,1,0:T(8,128)(2,1)S(1)} copy-done((bf16[24,128,128]{2,1,0:T(8,128)(2,1)S(1)}, bf16[24,128,128]{2,1,0:T(8,128)(2,1)}, u32[]{:S(2)}) %copy-start.1) | copy-done | bytes 786456
  28.0 1.2 %first_left.1 = (f32[2,768,384]{2,1,0:T(8,128)S(1)}, bf16[3,256,1024]{2,1,0:T(8,128)(2,1)S(1)}, bf16[384,384]{1,0:T(8,128)(2,1)S(1)}) custom-call(bf16[2,768,384]{2,1,0:T(8,128)(2,1)S(1)} %copy-done, bf16[24,128,128]{2,1,0:T(8,128)(2,1)S(1)} %copy-done.1), custom_call_target="tpu_custom_call" | custom-call | flops 1207959552 | bytes 8388608 | tf_op jit(solution)/shard_map/first_left/pallas_call | solution.py:281
  29.3 9.8 %collective-permute-done.2 = bf16[12,128,128]{2,1,0:T(8,128)(2,1)} collective-permute-done((bf16[12,128,128]{2,1,0:T(8,128)(2,1)}, bf16[12,128,128]{2,1,0:T(8,128)(2,1)}, u32[]{:S(2)}, u32[]{:S(2)}) %collective-permute-start.2) | collective-permute-done | bytes 393248 | tf_op jit(solution)/shard_map/ppermute | solution.py:279
  39.0 1.2 %maximum_select_fusion.halves = bf16[12,128,128]{2,1,0:T(8,128)(2,1)S(1)} fusion(bf16[12,128,128]{2,1,0:T(8,128)(2,1)} %collective-permute-done.2, bf16[6,128,128]{2,1,0:T(8,128)(2,1)} %collective-permute-done.3, pred[]{:T(512)S(6)} %eq.3), kind=kLoop, calls=%fused_computation.2 | loop fusion | flops 393216 | bytes 983041 | tf_op jit(solution)/shard_map/jit(_where)/select_n | solution.py:295
  40.2 1.9 %collective-permute-start.4 = (bf16[12,128,128]{2,1,0:T(8,128)(2,1)S(1)}, bf16[12,128,128]{2,1,0:T(8,128)(2,1)S(1)}, u32[]{:S(2)}, u32[]{:S(2)}) collective-permute-start(bf16[12,128,128]{2,1,0:T(8,128)(2,1)S(1)} %maximum_select_fusion.halves), channel_id=1, source_target_pairs={{0,32},{32,0},{64,96},{96,64},{128,160},{160,128},{192,224},{224,1... | collective-permute-start | bytes 1179656 | tf_op jit(solution)/shard_map/ppermute | solution.py:251
  42.2 1.7 %collective-permute-done.4.across = bf16[12,128,128]{2,1,0:T(8,128)(2,1)S(1)} collective-permute-done((bf16[12,128,128]{2,1,0:T(8,128)(2,1)S(1)}, bf16[12,128,128]{2,1,0:T(8,128)(2,1)S(1)}, u32[]{:S(2)}, u32[]{:S(2)}) %collective-permute-start.4) | collective-permute-done | bytes 393248 | tf_op jit(solution)/shard_map/ppermute | solution.py:251
  43.9 0.2 right_band.1.band
  44.1 10.6 %collective-permute-done.5.chip_far = bf16[1024,384]{1,0:T(8,128)(2,1)} collective-permute-done((bf16[1024,384]{1,0:T(8,128)(2,1)}, bf16[1024,384]{1,0:T(8,128)(2,1)}, u32[]{:S(2)}, u32[]{:S(2)}) %collective-permute-start.5) | collective-permute-done | bytes 786464 | tf_op jit(solution)/shard_map/ppermute | solution.py:256
  54.7 0.0 collective-permute-done.6.core_far
  54.7 0.0 collective-permute-done.1.after
  54.7 0.0 collective-permute-done.before
  54.7 4.4 %first_right.1 = (bf16[2,768,384]{2,1,0:T(8,128)(2,1)S(1)}, f32[2,768,384]{2,1,0:T(8,128)S(1)}, bf16[2,384,384]{2,1,0:T(8,128)(2,1)S(1)}, bf16[2,384,384]{2,1,0:T(8,128)(2,1)S(1)}, bf16[384,384]{1,0:T(8,128)(2,1)S(1)}) custom-call(bf16[2,768,384]{2,1,0:T(8,128)(2,1)S(1)} %collective-permute-done.before, bf16[2,768,384]{2,1,0:T(8,128)(2,1)S(1)} %copy-done, ...), custom_call_target="tpu_custom_call" | custom-call | flops 1358954496 | bytes 14680064 | tf_op jit(solution)/shard_map/first_right/pallas_call | solution.py:309
  59.2 1.9 %collective-permute-start.8 = (bf16[2,768,384]{2,1,0:T(8,128)(2,1)S(1)}, bf16[2,768,384]{2,1,0:T(8,128)(2,1)S(1)}, u32[]{:S(2)}, u32[]{:S(2)}) collective-permute-start(bf16[2,768,384]{2,1,0:T(8,128)(2,1)S(1)} %get-tuple-element.28.middle), channel_id=1, source_target_pairs={{1,0},{2,1},{3,2},{4,3},{5,4},{6,5},{7,6},{8,7},{9,8},{10,9},{11,1... | collective-permute-start | bytes 3538952 | tf_op jit(solution)/shard_map/ppermute | solution.py:41
  61.1 6.0 %collective-permute-start.7 = (bf16[2,768,384]{2,1,0:T(8,128)(2,1)S(1)}, bf16[2,768,384]{2,1,0:T(8,128)(2,1)S(1)}, u32[]{:S(2)}, u32[]{:S(2)}) collective-permute-start(bf16[2,768,384]{2,1,0:T(8,128)(2,1)S(1)} %get-tuple-element.28.middle), channel_id=1, source_target_pairs={{0,1},{1,2},{2,3},{3,4},{4,5},{5,6},{6,7},{7,8},{8,9},{9,10},{10,1... | collective-permute-start | bytes 3538952 | tf_op jit(solution)/shard_map/ppermute | solution.py:41
  67.1 4.6 %collective-permute-start.9 = (bf16[2,384,384]{2,1,0:T(8,128)(2,1)S(1)}, bf16[2,384,384]{2,1,0:T(8,128)(2,1)S(1)}, u32[]{:S(2)}, u32[]{:S(2)}) collective-permute-start(bf16[2,384,384]{2,1,0:T(8,128)(2,1)S(1)} %get-tuple-element.30), channel_id=1, source_target_pairs={{32,64},{96,128},{160,192},{224,256},{288,320},{352,384},{416,448}... | collective-permute-start | bytes 1769480 | tf_op jit(solution)/shard_map/ppermute | solution.py:256
  71.8 1.9 %collective-permute-start.10 = (bf16[2,384,384]{2,1,0:T(8,128)(2,1)S(1)}, bf16[2,384,384]{2,1,0:T(8,128)(2,1)S(1)}, u32[]{:S(2)}, u32[]{:S(2)}) collective-permute-start(bf16[2,384,384]{2,1,0:T(8,128)(2,1)S(1)} %get-tuple-element.31), channel_id=1, source_target_pairs={{0,32},{32,0},{64,96},{96,64},{128,160},{160,128},{192,224},{224,1... | collective-permute-start | bytes 1769480 | tf_op jit(solution)/shard_map/ppermute | solution.py:251
  73.7 1.8 %second_left.1.total = f32[2,768,384]{2,1,0:T(8,128)S(1)} custom-call(bf16[2,768,384]{2,1,0:T(8,128)(2,1)S(1)} %get-tuple-element.28.middle, bf16[3,256,1024]{2,1,0:T(8,128)(2,1)S(1)} %get-tuple-element.22.band, bf16[1152,384]{1,0:T(8,128)(2,1)S(1)} %right_band.1.band, f32[2,768,384]{2,1,0:T(8,128)S(1)} %get-tuple-element.29.total), custom_call_target="tpu_custom_call" | custom-call | flops 1660944384 | bytes 10485760 | tf_op jit(solution)/shard_map/second_left/pallas_call | solution.py:330
  75.5 28.1 %collective-permute-done.9.from_chip = bf16[2,384,384]{2,1,0:T(8,128)(2,1)S(1)} collective-permute-done((bf16[2,384,384]{2,1,0:T(8,128)(2,1)S(1)}, bf16[2,384,384]{2,1,0:T(8,128)(2,1)S(1)}, u32[]{:S(2)}, u32[]{:S(2)}) %collective-permute-start.9) | collective-permute-done | bytes 589856 | tf_op jit(solution)/shard_map/ppermute | solution.py:256
  103.6 0.0 collective-permute-done.10.from_core
  103.6 0.0 collective-permute-done.8.after
  103.6 0.0 collective-permute-done.7.before
  103.6 3.2 %last.1 = f32[2,768,384]{2,1,0:T(8,128)} custom-call(bf16[2,768,384]{2,1,0:T(8,128)(2,1)S(1)} %collective-permute-done.7.before, bf16[2,768,384]{2,1,0:T(8,128)(2,1)S(1)} %collective-permute-done.8.after, f32[2,768,384]{2,1,0:T(8,128)S(1)} %second_left.1.total, bf16[1152,384]{1,0:T(8,128)(2,1)S(1)} %right_band.1.band, ...), custom_call_target="tpu_custom_call" | custom-call | flops 905969664 | bytes 8388608 | tf_op jit(solution)/shard_map/last/pallas_call | solution.py:339
Async XLA Ops:
  0.0 54.7 %collective-permute-start.1 = (bf16[2,768,384]{2,1,0:T(8,128)(2,1)}, bf16[2,768,384]{2,1,0:T(8,128)(2,1)S(1)}, u32[]{:S(2)}, u32[]{:S(2)}) collective-permute-start(bf16[2,768,384]{2,1,0:T(8,128)(2,1)} %field.3), channel_id=1, source_target_pairs={{1,0},{2,1},{3,2},{4,3},{5,4},{6,5},{7,6},{8,7},{9,8},{10,9},{11,1... | collective-permute-start | bytes 3538952 | tf_op jit(solution)/shard_map/ppermute | solution.py:41
  2.5 52.3 %collective-permute-start = (bf16[2,768,384]{2,1,0:T(8,128)(2,1)}, bf16[2,768,384]{2,1,0:T(8,128)(2,1)S(1)}, u32[]{:S(2)}, u32[]{:S(2)}) collective-permute-start(bf16[2,768,384]{2,1,0:T(8,128)(2,1)} %field.3), channel_id=1, source_target_pairs={{0,1},{1,2},{2,3},{3,4},{4,5},{5,6},{6,7},{7,8},{8,9},{9,10},{10,1... | collective-permute-start | bytes 3538952 | tf_op jit(solution)/shard_map/ppermute | solution.py:41
  10.5 14.4 %collective-permute-start.3 = (bf16[6,128,128]{2,1,0:T(8,128)(2,1)}, bf16[6,128,128]{2,1,0:T(8,128)(2,1)}, u32[]{:S(2)}, u32[]{:S(2)}) collective-permute-start(bf16[6,128,128]{2,1,0:T(8,128)(2,1)} %get-tuple-element.24), channel_id=1, source_target_pairs={{0,97},{1,33},{2,226},{3,34},{8,225},{9,161},{10,162},{11,98},{16,... | collective-permute-start | bytes 589832 | tf_op jit(solution)/shard_map/ppermute | solution.py:280
  11.9 27.2 %collective-permute-start.2 = (bf16[12,128,128]{2,1,0:T(8,128)(2,1)}, bf16[12,128,128]{2,1,0:T(8,128)(2,1)}, u32[]{:S(2)}, u32[]{:S(2)}) collective-permute-start(bf16[12,128,128]{2,1,0:T(8,128)(2,1)} %get-tuple-element.21), channel_id=1, source_target_pairs={{0,192},{1,1},{2,129},{7,0},{8,128},{9,65},{10,193},{15,64},{16,44... | collective-permute-start | bytes 1179656 | tf_op jit(solution)/shard_map/ppermute | solution.py:279
  14.3 1.4 %copy-start.2 = (bf16[256,384]{1,0:T(8,128)(2,1)S(1)}, bf16[256,384]{1,0:T(8,128)(2,1)}, u32[]{:S(2)}) copy-start(bf16[256,384]{1,0:T(8,128)(2,1)} %get-tuple-element.25) | copy-start | bytes 589828
  15.7 11.1 %copy-start = (bf16[2,768,384]{2,1,0:T(8,128)(2,1)S(1)}, bf16[2,768,384]{2,1,0:T(8,128)(2,1)}, u32[]{:S(2)}) copy-start(bf16[2,768,384]{2,1,0:T(8,128)(2,1)} %field.3) | copy-start | bytes 3538948
  17.1 37.6 %collective-permute-start.5 = (bf16[1024,384]{1,0:T(8,128)(2,1)}, bf16[1024,384]{1,0:T(8,128)(2,1)}, u32[]{:S(2)}, u32[]{:S(2)}) collective-permute-start(bf16[1024,384]{1,0:T(8,128)(2,1)} %get-tuple-element.36), channel_id=1, source_target_pairs={{32,64},{96,128},{160,192},{224,256},{288,320},{352,384},{416,448}... | collective-permute-start | bytes 2359304 | tf_op jit(solution)/shard_map/ppermute | solution.py:256
  24.9 29.8 %collective-permute-start.6 = (bf16[1024,384]{1,0:T(8,128)(2,1)}, bf16[1024,384]{1,0:T(8,128)(2,1)}, u32[]{:S(2)}, u32[]{:S(2)}) collective-permute-start(bf16[1024,384]{1,0:T(8,128)(2,1)} %get-tuple-element.26), channel_id=1, source_target_pairs={{0,32},{32,0},{64,96},{96,64},{128,160},{160,128},{192,224},{224,1... | collective-permute-start | bytes 2359304 | tf_op jit(solution)/shard_map/ppermute | solution.py:251
  26.9 1.1 %copy-start.1 = (bf16[24,128,128]{2,1,0:T(8,128)(2,1)S(1)}, bf16[24,128,128]{2,1,0:T(8,128)(2,1)}, u32[]{:S(2)}) copy-start(bf16[24,128,128]{2,1,0:T(8,128)(2,1)} %get-tuple-element.19.upper) | copy-start | bytes 2359300
  40.2 3.6 %collective-permute-start.4 = (bf16[12,128,128]{2,1,0:T(8,128)(2,1)S(1)}, bf16[12,128,128]{2,1,0:T(8,128)(2,1)S(1)}, u32[]{:S(2)}, u32[]{:S(2)}) collective-permute-start(bf16[12,128,128]{2,1,0:T(8,128)(2,1)S(1)} %maximum_select_fusion.halves), channel_id=1, source_target_pairs={{0,32},{32,0},{64,96},{96,64},{128,160},{160,128},{192,224},{224,1... | collective-permute-start | bytes 1179656 | tf_op jit(solution)/shard_map/ppermute | solution.py:251
  59.2 44.5 %collective-permute-start.8 = (bf16[2,768,384]{2,1,0:T(8,128)(2,1)S(1)}, bf16[2,768,384]{2,1,0:T(8,128)(2,1)S(1)}, u32[]{:S(2)}, u32[]{:S(2)}) collective-permute-start(bf16[2,768,384]{2,1,0:T(8,128)(2,1)S(1)} %get-tuple-element.28.middle), channel_id=1, source_target_pairs={{1,0},{2,1},{3,2},{4,3},{5,4},{6,5},{7,6},{8,7},{9,8},{10,9},{11,1... | collective-permute-start | bytes 3538952 | tf_op jit(solution)/shard_map/ppermute | solution.py:41
  61.1 42.5 %collective-permute-start.7 = (bf16[2,768,384]{2,1,0:T(8,128)(2,1)S(1)}, bf16[2,768,384]{2,1,0:T(8,128)(2,1)S(1)}, u32[]{:S(2)}, u32[]{:S(2)}) collective-permute-start(bf16[2,768,384]{2,1,0:T(8,128)(2,1)S(1)} %get-tuple-element.28.middle), channel_id=1, source_target_pairs={{0,1},{1,2},{2,3},{3,4},{4,5},{5,6},{6,7},{7,8},{8,9},{9,10},{10,1... | collective-permute-start | bytes 3538952 | tf_op jit(solution)/shard_map/ppermute | solution.py:41
  67.1 36.5 %collective-permute-start.9 = (bf16[2,384,384]{2,1,0:T(8,128)(2,1)S(1)}, bf16[2,384,384]{2,1,0:T(8,128)(2,1)S(1)}, u32[]{:S(2)}, u32[]{:S(2)}) collective-permute-start(bf16[2,384,384]{2,1,0:T(8,128)(2,1)S(1)} %get-tuple-element.30), channel_id=1, source_target_pairs={{32,64},{96,128},{160,192},{224,256},{288,320},{352,384},{416,448}... | collective-permute-start | bytes 1769480 | tf_op jit(solution)/shard_map/ppermute | solution.py:256
  71.8 31.9 %collective-permute-start.10 = (bf16[2,384,384]{2,1,0:T(8,128)(2,1)S(1)}, bf16[2,384,384]{2,1,0:T(8,128)(2,1)S(1)}, u32[]{:S(2)}, u32[]{:S(2)}) collective-permute-start(bf16[2,384,384]{2,1,0:T(8,128)(2,1)S(1)} %get-tuple-element.31), channel_id=1, source_target_pairs={{0,32},{32,0},{64,96},{96,64},{128,160},{160,128},{192,224},{224,1... | collective-permute-start | bytes 1769480 | tf_op jit(solution)/shard_map/ppermute | solution.py:251

commit v3 on v2

--- a/solution.py
+++ b/solution.py
@@ -278,6 +278,8 @@
     to_core = edge(density, low, (1 - core_index()) * MARGIN)
     own = lax.ppermute(own, ("row", "col"), routes(0, OWN_CHIPS))
     crossing = lax.ppermute(crossing, ("row", "col"), routes(1, CROSSING_CHIPS))
+    halves = jnp.where(core_index() == 0, own, jnp.concatenate([crossing, crossing], axis=0))
+    across = to_other_core(halves)
     left, left_band, below_band = pl.pallas_call(
         first_left_kernel,
         in_specs=[VMEM] * 2,
@@ -291,10 +293,7 @@
         cost_estimate=cost(2 * TALL * 1024 * 2 * WIDE, 8 * MIB),
         name="first_left",
     )(density, upper)
-    own, _ = lax.optimization_barrier((own, left_band))
-    halves = jnp.where(core_index() == 0, own, jnp.concatenate([crossing, crossing], axis=0))
-    across = to_other_core(halves)
-    to_core, _ = lax.optimization_barrier((to_core, crossing))
+    to_core, _, _ = lax.optimization_barrier((to_core, crossing, left_band))
     from_chip = to_other_chip(to_chip)
     from_core = to_other_core(to_core)
     right_band = pl.pallas_call(

time: 107 us -> 108 us (level)
  transfers between devices with their start and end apart: 11 -> 11, of which waited for: 4 -> 4; matrix products, arithmetic and copies ran while one was open for 4% -> 4% of each run, Pallas kernels for 6% -> 5%
where the time goes in v3:
time: 108 us; the launch traced here: 107 us
  waiting for transfers between devices  49.5 us (46%)
  starting transfers between devices  38 us (35%)
  Pallas kernels  14 us (13%)
  local copies, waits for them, and re-layouts  3.26 us (3%)
  other arithmetic  2.52 us (2%)
    ppermute x2, waiting for transfers between devices, to_other_chip(): return lax.ppermute(block, 'row', ends + [(j, i) for i, j in ends])  38.9 us
    ppermute x4, starting transfers between devices, to_column(): lax.ppermute(block, 'col', [(i - distance, i) for i in range(COLS) if 0 <...  15.9 us
    ppermute x2, starting transfers between devices, to_other_chip(): return lax.ppermute(block, 'row', ends + [(j, i) for i, j in ends])  12.5 us
    ppermute x1, waiting for transfers between devices, on_device(): own = lax.ppermute(own, ('row', 'col'), routes(0, OWN_CHIPS))  8.92 us
    ppermute x3, starting transfers between devices, to_other_core(): return lax.ppermute(block, 'row', [(i, i ^ 1) for i in range(ROWS)])  5.75 us
    pallas_call x1, Pallas kernels, on_device(): pl.pallas_call(first_right_kernel, in_specs=[VMEM] * 5 + [any_space] * 2...  4.94 us
    pallas_call x1, Pallas kernels, on_device(): pl.pallas_call(last_kernel, in_specs=[VMEM] * 8, out_specs=any_space, out...  3.17 us
    pallas_call x1, Pallas kernels, on_device(): pl.pallas_call(start_kernel, in_specs=[VMEM] * 2, out_specs=[VMEM] * 4, o...  2.59 us
  transfers between devices with their start and end apart: 11, of which 4 were waited for; matrix products, arithmetic and copies ran while one was open for 4% of the time, Pallas kernels for 5%

profile of v3, /device:TPU:496, one launch (start us, length us, event | category | flops | bytes accessed | tf_op | source)
XLA Modules:
  0.0 107.5 jit_solution(462921977444186114)
XLA Ops:
  0.0 2.5 %collective-permute-start.1 = (bf16[2,768,384]{2,1,0:T(8,128)(2,1)}, bf16[2,768,384]{2,1,0:T(8,128)(2,1)}, u32[]{:S(2)}, u32[]{:S(2)}) collective-permute-start(bf16[2,768,384]{2,1,0:T(8,128)(2,1)} %field.3), channel_id=1, source_target_pairs={{1,0},{2,1},{3,2},{4,3},{5,4},{6,5},{7,6},{8,7},{9,8},{10,9},{11,1... | collective-permute-start | bytes 3538952 | tf_op jit(solution)/shard_map/ppermute | solution.py:41
  2.5 5.5 %collective-permute-start = (bf16[2,768,384]{2,1,0:T(8,128)(2,1)}, bf16[2,768,384]{2,1,0:T(8,128)(2,1)}, u32[]{:S(2)}, u32[]{:S(2)}) collective-permute-start(bf16[2,768,384]{2,1,0:T(8,128)(2,1)} %field.3), channel_id=1, source_target_pairs={{0,1},{1,2},{2,3},{3,4},{4,5},{5,6},{6,7},{7,8},{8,9},{9,10},{10,1... | collective-permute-start | bytes 3538952 | tf_op jit(solution)/shard_map/ppermute | solution.py:41
  8.0 2.6 %start.1 = (bf16[24,128,128]{2,1,0:T(8,128)(2,1)}, bf16[12,128,128]{2,1,0:T(8,128)(2,1)}, bf16[6,128,128]{2,1,0:T(8,128)(2,1)}, bf16[256,384]{1,0:T(8,128)(2,1)}) custom-call(s32[4,6]{1,0:T(4,128)} %bitcast.5, bf16[6,4,128,128]{3,2,1,0:T(8,128)(2,1)} %hvals.1), custom_call_target="tpu_custom_call" | custom-call | bytes 2097152 | tf_op jit(solution)/shard_map/start/pallas_call | solution.py:263
  10.6 0.0 copy-start.6
  10.6 1.5 %collective-permute-start.3 = (bf16[6,128,128]{2,1,0:T(8,128)(2,1)}, bf16[6,128,128]{2,1,0:T(8,128)(2,1)}, u32[]{:S(2)}, u32[]{:S(2)}) collective-permute-start(bf16[6,128,128]{2,1,0:T(8,128)(2,1)} %get-tuple-element.21), channel_id=1, source_target_pairs={{0,97},{1,33},{2,226},{3,34},{8,225},{9,161},{10,162},{11,98},{16,... | collective-permute-start | bytes 589832 | tf_op jit(solution)/shard_map/ppermute | solution.py:280
  12.0 2.4 %collective-permute-start.2 = (bf16[12,128,128]{2,1,0:T(8,128)(2,1)}, bf16[12,128,128]{2,1,0:T(8,128)(2,1)}, u32[]{:S(2)}, u32[]{:S(2)}) collective-permute-start(bf16[12,128,128]{2,1,0:T(8,128)(2,1)} %get-tuple-element.20), channel_id=1, source_target_pairs={{0,192},{1,1},{2,129},{7,0},{8,128},{9,65},{10,193},{15,64},{16,44... | collective-permute-start | bytes 1179656 | tf_op jit(solution)/shard_map/ppermute | solution.py:279
  14.5 1.4 %constant_dynamic-slice_fusion = (bf16[2,384,384]{2,1,0:T(8,128)(2,1)S(1)}, bf16[2,384,384]{2,1,0:T(8,128)(2,1)S(1)}) fusion(bf16[2,768,384]{2,1,0:T(8,128)(2,1)} %field.3, s32[]{:T(128)S(6)} %select_n.17, s32[]{:T(128)S(6)} %select_n.16), kind=kLoop, calls=%fused_computation.3 | loop fusion | bytes 2359304 | tf_op jit(solution)/shard_map/dynamic_slice | solution.py:98
  15.8 0.0 copy-start
  15.9 0.0 copy-start.5
  15.9 0.0 copy-done.6
  15.9 1.3 %pad_maximum_fusion = (bf16[1024,384]{1,0:T(8,128)(2,1)}, bf16[1024,384]{1,0:T(8,128)(2,1)}) fusion(bf16[256,384]{1,0:T(8,128)(2,1)S(1)} %copy-done.6, bf16[768,384]{1,0:T(8,128)(2,1)S(1)} %bitcast.3, bf16[768,384]{1,0:T(8,128)(2,1)S(1)} %bitcast.4), kind=kLoop, calls=%fused_computation | loop fusion | flops 2752512 | bytes 2949120 | tf_op jit(solution)/shard_map/concatenate | solution.py:99
  17.2 7.8 %collective-permute-start.5 = (bf16[1024,384]{1,0:T(8,128)(2,1)}, bf16[1024,384]{1,0:T(8,128)(2,1)}, u32[]{:S(2)}, u32[]{:S(2)}) collective-permute-start(bf16[1024,384]{1,0:T(8,128)(2,1)} %get-tuple-element.34), channel_id=1, source_target_pairs={{32,64},{96,128},{160,192},{224,256},{288,320},{352,384},{416,448}... | collective-permute-start | bytes 2359304 | tf_op jit(solution)/shard_map/ppermute | solution.py:256
  25.0 0.0 copy-done
  25.1 0.0 copy-done.5
  25.1 1.2 %first_left.1 = (f32[2,768,384]{2,1,0:T(8,128)S(1)}, bf16[3,256,1024]{2,1,0:T(8,128)(2,1)S(1)}, bf16[384,384]{1,0:T(8,128)(2,1)S(1)}) custom-call(bf16[2,768,384]{2,1,0:T(8,128)(2,1)S(1)} %copy-done, bf16[24,128,128]{2,1,0:T(8,128)(2,1)S(1)} %copy-done.5), custom_call_target="tpu_custom_call" | custom-call | flops 1207959552 | bytes 8388608 | tf_op jit(solution)/shard_map/first_left/pallas_call | solution.py:283
  26.3 0.0 copy-start.1
  26.3 1.1 %copy-done.1 = bf16[3,256,1024]{2,1,0:T(8,128)(2,1)} copy-done((bf16[3,256,1024]{2,1,0:T(8,128)(2,1)}, bf16[3,256,1024]{2,1,0:T(8,128)(2,1)S(1)}, u32[]{:S(2)}) %copy-start.1) | copy-done | bytes 1572888
  27.5 0.0 copy-start.3
  27.5 0.7 copy-done.3
  28.2 0.0 collective-permute-done.3
  28.2 1.9 %collective-permute-start.6 = (bf16[1024,384]{1,0:T(8,128)(2,1)}, bf16[1024,384]{1,0:T(8,128)(2,1)}, u32[]{:S(2)}, u32[]{:S(2)}) collective-permute-start(bf16[1024,384]{1,0:T(8,128)(2,1)} %get-tuple-element.24), channel_id=1, source_target_pairs={{0,32},{32,0},{64,96},{96,64},{128,160},{160,128},{192,224},{224,1... | collective-permute-start | bytes 2359304 | tf_op jit(solution)/shard_map/ppermute | solution.py:251
  30.1 0.0 copy-start.4
  30.1 8.9 %collective-permute-done.2 = bf16[12,128,128]{2,1,0:T(8,128)(2,1)} collective-permute-done((bf16[12,128,128]{2,1,0:T(8,128)(2,1)}, bf16[12,128,128]{2,1,0:T(8,128)(2,1)}, u32[]{:S(2)}, u32[]{:S(2)}) %collective-permute-start.2) | collective-permute-done | bytes 393248 | tf_op jit(solution)/shard_map/ppermute | solution.py:279
  39.0 1.2 %maximum_select_fusion.halves = bf16[12,128,128]{2,1,0:T(8,128)(2,1)S(1)} fusion(bf16[12,128,128]{2,1,0:T(8,128)(2,1)} %collective-permute-done.2, bf16[6,128,128]{2,1,0:T(8,128)(2,1)} %collective-permute-done.3, pred[]{:T(512)S(6)} %eq.3), kind=kLoop, calls=%fused_computation.2 | loop fusion | flops 393216 | bytes 983041 | tf_op jit(solution)/shard_map/jit(_where)/select_n | solution.py:281
  40.2 1.9 %collective-permute-start.4 = (bf16[12,128,128]{2,1,0:T(8,128)(2,1)S(1)}, bf16[12,128,128]{2,1,0:T(8,128)(2,1)S(1)}, u32[]{:S(2)}, u32[]{:S(2)}) collective-permute-start(bf16[12,128,128]{2,1,0:T(8,128)(2,1)S(1)} %maximum_select_fusion.halves), channel_id=1, source_target_pairs={{0,32},{32,0},{64,96},{96,64},{128,160},{160,128},{192,224},{224,1... | collective-permute-start | bytes 1179656 | tf_op jit(solution)/shard_map/ppermute | solution.py:251
  42.2 1.7 %collective-permute-done.4.across = bf16[12,128,128]{2,1,0:T(8,128)(2,1)S(1)} collective-permute-done((bf16[12,128,128]{2,1,0:T(8,128)(2,1)S(1)}, bf16[12,128,128]{2,1,0:T(8,128)(2,1)S(1)}, u32[]{:S(2)}, u32[]{:S(2)}) %collective-permute-start.4) | collective-permute-done | bytes 393248 | tf_op jit(solution)/shard_map/ppermute | solution.py:251
  43.9 0.2 right_band.1.band
  44.1 10.6 %collective-permute-done.5.chip_far = bf16[1024,384]{1,0:T(8,128)(2,1)} collective-permute-done((bf16[1024,384]{1,0:T(8,128)(2,1)}, bf16[1024,384]{1,0:T(8,128)(2,1)}, u32[]{:S(2)}, u32[]{:S(2)}) %collective-permute-start.5) | collective-permute-done | bytes 786464 | tf_op jit(solution)/shard_map/ppermute | solution.py:256
  54.7 0.0 collective-permute-done.6.core_far
  54.7 0.0 collective-permute-done.1.after
  54.7 0.0 collective-permute-done.before
  54.7 0.0 copy-done.4
  54.7 0.0 copy-start.2
  54.7 4.9 %first_right.1 = (bf16[2,768,384]{2,1,0:T(8,128)(2,1)S(1)}, f32[2,768,384]{2,1,0:T(8,128)S(1)}, bf16[2,384,384]{2,1,0:T(8,128)(2,1)S(1)}, bf16[2,384,384]{2,1,0:T(8,128)(2,1)S(1)}, bf16[384,384]{1,0:T(8,128)(2,1)S(1)}) custom-call(bf16[2,768,384]{2,1,0:T(8,128)(2,1)} %collective-permute-done.before, bf16[2,768,384]{2,1,0:T(8,128)(2,1)S(1)} %copy-done, ...), custom_call_target="tpu_custom_call" | custom-call | flops 1358954496 | bytes 14680064 | tf_op jit(solution)/shard_map/first_right/pallas_call | solution.py:308
  59.7 1.9 %collective-permute-start.8 = (bf16[2,768,384]{2,1,0:T(8,128)(2,1)S(1)}, bf16[2,768,384]{2,1,0:T(8,128)(2,1)S(1)}, u32[]{:S(2)}, u32[]{:S(2)}) collective-permute-start(bf16[2,768,384]{2,1,0:T(8,128)(2,1)S(1)} %get-tuple-element.26.middle), channel_id=1, source_target_pairs={{1,0},{2,1},{3,2},{4,3},{5,4},{6,5},{7,6},{8,7},{9,8},{10,9},{11,1... | collective-permute-start | bytes 3538952 | tf_op jit(solution)/shard_map/ppermute | solution.py:41
  61.6 6.0 %collective-permute-start.7 = (bf16[2,768,384]{2,1,0:T(8,128)(2,1)S(1)}, bf16[2,768,384]{2,1,0:T(8,128)(2,1)S(1)}, u32[]{:S(2)}, u32[]{:S(2)}) collective-permute-start(bf16[2,768,384]{2,1,0:T(8,128)(2,1)S(1)} %get-tuple-element.26.middle), channel_id=1, source_target_pairs={{0,1},{1,2},{2,3},{3,4},{4,5},{5,6},{6,7},{7,8},{8,9},{9,10},{10,1... | collective-permute-start | bytes 3538952 | tf_op jit(solution)/shard_map/ppermute | solution.py:41
  67.7 4.6 %collective-permute-start.9 = (bf16[2,384,384]{2,1,0:T(8,128)(2,1)S(1)}, bf16[2,384,384]{2,1,0:T(8,128)(2,1)S(1)}, u32[]{:S(2)}, u32[]{:S(2)}) collective-permute-start(bf16[2,384,384]{2,1,0:T(8,128)(2,1)S(1)} %get-tuple-element.28), channel_id=1, source_target_pairs={{32,64},{96,128},{160,192},{224,256},{288,320},{352,384},{416,448}... | collective-permute-start | bytes 1769480 | tf_op jit(solution)/shard_map/ppermute | solution.py:256
  72.3 1.9 %collective-permute-start.10 = (bf16[2,384,384]{2,1,0:T(8,128)(2,1)S(1)}, bf16[2,384,384]{2,1,0:T(8,128)(2,1)S(1)}, u32[]{:S(2)}, u32[]{:S(2)}) collective-permute-start(bf16[2,384,384]{2,1,0:T(8,128)(2,1)S(1)} %get-tuple-element.29), channel_id=1, source_target_pairs={{0,32},{32,0},{64,96},{96,64},{128,160},{160,128},{192,224},{224,1... | collective-permute-start | bytes 1769480 | tf_op jit(solution)/shard_map/ppermute | solution.py:251
  74.2 0.0 copy-done.2
  74.2 1.8 %second_left.1.total = f32[2,768,384]{2,1,0:T(8,128)S(1)} custom-call(bf16[2,768,384]{2,1,0:T(8,128)(2,1)S(1)} %get-tuple-element.26.middle, bf16[3,256,1024]{2,1,0:T(8,128)(2,1)S(1)} %copy-done.2, bf16[1152,384]{1,0:T(8,128)(2,1)S(1)} %right_band.1.band, f32[2,768,384]{2,1,0:T(8,128)S(1)} %get-tuple-element.27.total), custom_call_target="tpu_custom_call" | custom-call | flops 1660944384 | bytes 10485760 | tf_op jit(solution)/shard_map/second_left/pallas_call | solution.py:329
  76.0 28.2 %collective-permute-done.9.from_chip = bf16[2,384,384]{2,1,0:T(8,128)(2,1)S(1)} collective-permute-done((bf16[2,384,384]{2,1,0:T(8,128)(2,1)S(1)}, bf16[2,384,384]{2,1,0:T(8,128)(2,1)S(1)}, u32[]{:S(2)}, u32[]{:S(2)}) %collective-permute-start.9) | collective-permute-done | bytes 589856 | tf_op jit(solution)/shard_map/ppermute | solution.py:256
  104.3 0.0 collective-permute-done.10.from_core
  104.3 0.0 collective-permute-done.8.after
  104.3 0.0 collective-permute-done.7.before
  104.3 3.2 %last.1 = f32[2,768,384]{2,1,0:T(8,128)} custom-call(bf16[2,768,384]{2,1,0:T(8,128)(2,1)S(1)} %collective-permute-done.7.before, bf16[2,768,384]{2,1,0:T(8,128)(2,1)S(1)} %collective-permute-done.8.after, f32[2,768,384]{2,1,0:T(8,128)S(1)} %second_left.1.total, bf16[1152,384]{1,0:T(8,128)(2,1)S(1)} %right_band.1.band, ...), custom_call_target="tpu_custom_call" | custom-call | flops 905969664 | bytes 8388608 | tf_op jit(solution)/shard_map/last/pallas_call | solution.py:338
Async XLA Ops:
  0.0 54.7 %collective-permute-start.1 = (bf16[2,768,384]{2,1,0:T(8,128)(2,1)}, bf16[2,768,384]{2,1,0:T(8,128)(2,1)}, u32[]{:S(2)}, u32[]{:S(2)}) collective-permute-start(bf16[2,768,384]{2,1,0:T(8,128)(2,1)} %field.3), channel_id=1, source_target_pairs={{1,0},{2,1},{3,2},{4,3},{5,4},{6,5},{7,6},{8,7},{9,8},{10,9},{11,1... | collective-permute-start | bytes 3538952 | tf_op jit(solution)/shard_map/ppermute | solution.py:41
  2.5 52.3 %collective-permute-start = (bf16[2,768,384]{2,1,0:T(8,128)(2,1)}, bf16[2,768,384]{2,1,0:T(8,128)(2,1)}, u32[]{:S(2)}, u32[]{:S(2)}) collective-permute-start(bf16[2,768,384]{2,1,0:T(8,128)(2,1)} %field.3), channel_id=1, source_target_pairs={{0,1},{1,2},{2,3},{3,4},{4,5},{5,6},{6,7},{7,8},{8,9},{9,10},{10,1... | collective-permute-start | bytes 3538952 | tf_op jit(solution)/shard_map/ppermute | solution.py:41
  10.6 5.3 %copy-start.6 = (bf16[256,384]{1,0:T(8,128)(2,1)S(1)}, bf16[256,384]{1,0:T(8,128)(2,1)}, u32[]{:S(2)}) copy-start(bf16[256,384]{1,0:T(8,128)(2,1)} %get-tuple-element.22) | copy-start | bytes 589828
  10.6 17.6 %collective-permute-start.3 = (bf16[6,128,128]{2,1,0:T(8,128)(2,1)}, bf16[6,128,128]{2,1,0:T(8,128)(2,1)}, u32[]{:S(2)}, u32[]{:S(2)}) collective-permute-start(bf16[6,128,128]{2,1,0:T(8,128)(2,1)} %get-tuple-element.21), channel_id=1, source_target_pairs={{0,97},{1,33},{2,226},{3,34},{8,225},{9,161},{10,162},{11,98},{16,... | collective-permute-start | bytes 589832 | tf_op jit(solution)/shard_map/ppermute | solution.py:280
  12.0 27.0 %collective-permute-start.2 = (bf16[12,128,128]{2,1,0:T(8,128)(2,1)}, bf16[12,128,128]{2,1,0:T(8,128)(2,1)}, u32[]{:S(2)}, u32[]{:S(2)}) collective-permute-start(bf16[12,128,128]{2,1,0:T(8,128)(2,1)} %get-tuple-element.20), channel_id=1, source_target_pairs={{0,192},{1,1},{2,129},{7,0},{8,128},{9,65},{10,193},{15,64},{16,44... | collective-permute-start | bytes 1179656 | tf_op jit(solution)/shard_map/ppermute | solution.py:279
  15.8 9.2 %copy-start = (bf16[2,768,384]{2,1,0:T(8,128)(2,1)S(1)}, bf16[2,768,384]{2,1,0:T(8,128)(2,1)}, u32[]{:S(2)}) copy-start(bf16[2,768,384]{2,1,0:T(8,128)(2,1)} %field.3) | copy-start | bytes 3538948
  15.9 9.2 %copy-start.5 = (bf16[24,128,128]{2,1,0:T(8,128)(2,1)S(1)}, bf16[24,128,128]{2,1,0:T(8,128)(2,1)}, u32[]{:S(2)}) copy-start(bf16[24,128,128]{2,1,0:T(8,128)(2,1)} %get-tuple-element.18.upper) | copy-start | bytes 2359300
  17.2 37.5 %collective-permute-start.5 = (bf16[1024,384]{1,0:T(8,128)(2,1)}, bf16[1024,384]{1,0:T(8,128)(2,1)}, u32[]{:S(2)}, u32[]{:S(2)}) collective-permute-start(bf16[1024,384]{1,0:T(8,128)(2,1)} %get-tuple-element.34), channel_id=1, source_target_pairs={{32,64},{96,128},{160,192},{224,256},{288,320},{352,384},{416,448}... | collective-permute-start | bytes 2359304 | tf_op jit(solution)/shard_map/ppermute | solution.py:256
  26.3 1.1 %copy-start.1 = (bf16[3,256,1024]{2,1,0:T(8,128)(2,1)}, bf16[3,256,1024]{2,1,0:T(8,128)(2,1)S(1)}, u32[]{:S(2)}) copy-start(bf16[3,256,1024]{2,1,0:T(8,128)(2,1)S(1)} %get-tuple-element.23.band) | copy-start | bytes 4718596
  27.5 0.7 copy-start.3
  28.2 26.5 %collective-permute-start.6 = (bf16[1024,384]{1,0:T(8,128)(2,1)}, bf16[1024,384]{1,0:T(8,128)(2,1)}, u32[]{:S(2)}, u32[]{:S(2)}) collective-permute-start(bf16[1024,384]{1,0:T(8,128)(2,1)} %get-tuple-element.24), channel_id=1, source_target_pairs={{0,32},{32,0},{64,96},{96,64},{128,160},{160,128},{192,224},{224,1... | collective-permute-start | bytes 2359304 | tf_op jit(solution)/shard_map/ppermute | solution.py:251
  30.1 24.6 %copy-start.4 = (bf16[384,384]{1,0:T(8,128)(2,1)S(1)}, bf16[384,384]{1,0:T(8,128)(2,1)}, u32[]{:S(2)}) copy-start(bf16[384,384]{1,0:T(8,128)(2,1)} %copy-done.3) | copy-start | bytes 884740
  40.2 3.6 %collective-permute-start.4 = (bf16[12,128,128]{2,1,0:T(8,128)(2,1)S(1)}, bf16[12,128,128]{2,1,0:T(8,128)(2,1)S(1)}, u32[]{:S(2)}, u32[]{:S(2)}) collective-permute-start(bf16[12,128,128]{2,1,0:T(8,128)(2,1)S(1)} %maximum_select_fusion.halves), channel_id=1, source_target_pairs={{0,32},{32,0},{64,96},{96,64},{128,160},{160,128},{192,224},{224,1... | collective-permute-start | bytes 1179656 | tf_op jit(solution)/shard_map/ppermute | solution.py:251
  54.7 19.5 %copy-start.2 = (bf16[3,256,1024]{2,1,0:T(8,128)(2,1)S(1)}, bf16[3,256,1024]{2,1,0:T(8,128)(2,1)}, u32[]{:S(2)}) copy-start(bf16[3,256,1024]{2,1,0:T(8,128)(2,1)} %copy-done.1) | copy-start | bytes 4718596
  59.7 44.6 %collective-permute-start.8 = (bf16[2,768,384]{2,1,0:T(8,128)(2,1)S(1)}, bf16[2,768,384]{2,1,0:T(8,128)(2,1)S(1)}, u32[]{:S(2)}, u32[]{:S(2)}) collective-permute-start(bf16[2,768,384]{2,1,0:T(8,128)(2,1)S(1)} %get-tuple-element.26.middle), channel_id=1, source_target_pairs={{1,0},{2,1},{3,2},{4,3},{5,4},{6,5},{7,6},{8,7},{9,8},{10,9},{11,1... | collective-permute-start | bytes 3538952 | tf_op jit(solution)/shard_map/ppermute | solution.py:41
  61.6 42.7 %collective-permute-start.7 = (bf16[2,768,384]{2,1,0:T(8,128)(2,1)S(1)}, bf16[2,768,384]{2,1,0:T(8,128)(2,1)S(1)}, u32[]{:S(2)}, u32[]{:S(2)}) collective-permute-start(bf16[2,768,384]{2,1,0:T(8,128)(2,1)S(1)} %get-tuple-element.26.middle), channel_id=1, source_target_pairs={{0,1},{1,2},{2,3},{3,4},{4,5},{5,6},{6,7},{7,8},{8,9},{9,10},{10,1... | collective-permute-start | bytes 3538952 | tf_op jit(solution)/shard_map/ppermute | solution.py:41
  67.7 36.6 %collective-permute-start.9 = (bf16[2,384,384]{2,1,0:T(8,128)(2,1)S(1)}, bf16[2,384,384]{2,1,0:T(8,128)(2,1)S(1)}, u32[]{:S(2)}, u32[]{:S(2)}) collective-permute-start(bf16[2,384,384]{2,1,0:T(8,128)(2,1)S(1)} %get-tuple-element.28), channel_id=1, source_target_pairs={{32,64},{96,128},{160,192},{224,256},{288,320},{352,384},{416,448}... | collective-permute-start | bytes 1769480 | tf_op jit(solution)/shard_map/ppermute | solution.py:256
  72.3 32.0 %collective-permute-start.10 = (bf16[2,384,384]{2,1,0:T(8,128)(2,1)S(1)}, bf16[2,384,384]{2,1,0:T(8,128)(2,1)S(1)}, u32[]{:S(2)}, u32[]{:S(2)}) collective-permute-start(bf16[2,384,384]{2,1,0:T(8,128)(2,1)S(1)} %get-tuple-element.29), channel_id=1, source_target_pairs={{0,32},{32,0},{64,96},{96,64},{128,160},{160,128},{192,224},{224,1... | collective-permute-start | bytes 1769480 | tf_op jit(solution)/shard_map/ppermute | solution.py:251

commit v4 on v2

--- a/solution.py
+++ b/solution.py
@@ -163,30 +163,10 @@
 
 
 def first_right_kernel(
-    before, field, after, left, band, chip_far, core_far, below_band,
-    middle, total, to_chip, to_core, above_band, from_chip, from_core, sems,
+    before, field, after, left, band, from_chip, from_core, below_band,
+    middle, total, to_chip, to_core, above_band,
 ):
     core = core_index()
-    copies = [
-        pltpu.make_async_copy(far, near, sems.at[k])
-        for k, (far, near) in enumerate(((chip_far, from_chip), (core_far, from_core)))
-    ]
-    for copy in copies:
-        copy.start()
-    for part in range(2):
-        for k in range(2):
-            rows = slice(k * MARGIN, (k + 1) * MARGIN)
-            stretch = jnp.concatenate([before[part, rows], field[part, rows], after[part, rows]], axis=1)
-            product = jnp.concatenate(
-                [
-                    jnp.dot(stretch[:, :1024], band[:1024, :256], preferred_element_type=F32),
-                    jnp.dot(stretch[:, 256:], band[256:, 256:], preferred_element_type=F32),
-                ],
-                axis=1,
-            )
-            total[1 - part, rows] = left[part, rows] - product
-    for copy in copies:
-        copy.wait()
     for i in range(3):
         for c in range(3):
             block = jnp.zeros((BLK, BLK), BF16)
@@ -205,8 +185,16 @@
         )
         for k, (outer, beyond) in enumerate(halves):
             rows = slice(k * MARGIN, (k + 1) * MARGIN)
+            stretch = jnp.concatenate([before[part, rows], field[part, rows], after[part, rows]], axis=1)
+            product = jnp.concatenate(
+                [
+                    jnp.dot(stretch[:, :1024], band[:1024, :256], preferred_element_type=F32),
+                    jnp.dot(stretch[:, 256:], band[256:, 256:], preferred_element_type=F32),
+                ],
+                axis=1,
+            )
             far = jnp.dot(outer[...], beyond, preferred_element_type=F32)
-            rate = sign * (total[other, rows] + far)
+            rate = sign * (left[part, rows] + far - product)
             start = field[other, rows].astype(F32)
             middle[other, rows] = (start + DT * rate).astype(BF16)
             total[other, rows] = start + (DT / 2) * rate
@@ -308,7 +296,7 @@
     )(halves, across)
     middle, total, to_chip, to_core, above_band = pl.pallas_call(
         first_right_kernel,
-        in_specs=[VMEM] * 5 + [any_space] * 2 + [VMEM],
+        in_specs=[VMEM] * 8,
         out_specs=[VMEM] * 5,
         out_shape=[
             jax.ShapeDtypeStruct((2, TALL, WIDE), BF16),
@@ -317,7 +305,6 @@
             jax.ShapeDtypeStruct((2, MARGIN, WIDE), BF16),
             jax.ShapeDtypeStruct((MARGIN, MARGIN), BF16),
         ],
-        scratch_shapes=[pltpu.VMEM((2 * MARGIN + 2 * BLK, WIDE), BF16)] * 2 + [pltpu.SemaphoreType.DMA((2,))],
         compiler_params=params(20),
         cost_estimate=cost(4 * TALL * 9 * BLK * WIDE, 14 * MIB),
         name="first_right",

time: 107 us -> 107 us (level)
  no operation moved by 1% of the time
where the time goes in v4:
time: 107 us
  waiting for transfers between devices  50.2 us (47%)
  starting transfers between devices  37.8 us (35%)
  Pallas kernels  13.3 us (12%)
  local copies, waits for them, and re-layouts  2.55 us (2%)
  other arithmetic  2.51 us (2%)
    ppermute x2, waiting for transfers between devices, to_other_chip(): return lax.ppermute(block, 'row', ends + [(j, i) for i, j in ends])  38.7 us
    ppermute x4, starting transfers between devices, to_column(): lax.ppermute(block, 'col', [(i - distance, i) for i in range(COLS) if 0 <...  15.9 us
    ppermute x2, starting transfers between devices, to_other_chip(): return lax.ppermute(block, 'row', ends + [(j, i) for i, j in ends])  12.4 us
    ppermute x1, waiting for transfers between devices, on_device(): own = lax.ppermute(own, ('row', 'col'), routes(0, OWN_CHIPS))  9.79 us
    ppermute x3, starting transfers between devices, to_other_core(): return lax.ppermute(block, 'row', [(i, i ^ 1) for i in range(ROWS)])  5.76 us
    pallas_call x1, Pallas kernels, on_device(): pl.pallas_call(first_right_kernel, in_specs=[VMEM] * 8, out_specs=[VMEM]...  4.26 us
    pallas_call x1, Pallas kernels, on_device(): pl.pallas_call(last_kernel, in_specs=[VMEM] * 8, out_specs=any_space, out...  3.17 us
    pallas_call x1, Pallas kernels, on_device(): pl.pallas_call(start_kernel, in_specs=[VMEM] * 2, out_specs=[VMEM] * 4, o...  2.58 us
  transfers between devices with their start and end apart: 11, of which 4 were waited for; matrix products, arithmetic and copies ran while one was open for 4% of the time, Pallas kernels for 6%

profile of v4, /device:TPU:496, one launch (start us, length us, event | category | flops | bytes accessed | tf_op | source)
XLA Modules:
  0.0 106.6 jit_solution(16235324897940254738)
XLA Ops:
  0.0 2.5 %collective-permute-start.1 = (bf16[2,768,384]{2,1,0:T(8,128)(2,1)}, bf16[2,768,384]{2,1,0:T(8,128)(2,1)S(1)}, u32[]{:S(2)}, u32[]{:S(2)}) collective-permute-start(bf16[2,768,384]{2,1,0:T(8,128)(2,1)} %field.3), channel_id=1, source_target_pairs={{1,0},{2,1},{3,2},{4,3},{5,4},{6,5},{7,6},{8,7},{9,8},{10,9},{11,1... | collective-permute-start | bytes 3538952 | tf_op jit(solution)/shard_map/ppermute | solution.py:41
  2.5 5.5 %collective-permute-start = (bf16[2,768,384]{2,1,0:T(8,128)(2,1)}, bf16[2,768,384]{2,1,0:T(8,128)(2,1)S(1)}, u32[]{:S(2)}, u32[]{:S(2)}) collective-permute-start(bf16[2,768,384]{2,1,0:T(8,128)(2,1)} %field.3), channel_id=1, source_target_pairs={{0,1},{1,2},{2,3},{3,4},{4,5},{5,6},{6,7},{7,8},{8,9},{9,10},{10,1... | collective-permute-start | bytes 3538952 | tf_op jit(solution)/shard_map/ppermute | solution.py:41
  8.0 2.6 %start.1 = (bf16[24,128,128]{2,1,0:T(8,128)(2,1)}, bf16[12,128,128]{2,1,0:T(8,128)(2,1)}, bf16[6,128,128]{2,1,0:T(8,128)(2,1)}, bf16[256,384]{1,0:T(8,128)(2,1)}) custom-call(s32[4,6]{1,0:T(4,128)} %bitcast.5, bf16[6,4,128,128]{3,2,1,0:T(8,128)(2,1)} %hvals.1), custom_call_target="tpu_custom_call" | custom-call | bytes 2097152 | tf_op jit(solution)/shard_map/start/pallas_call | solution.py:251
  10.5 1.3 %collective-permute-start.3 = (bf16[6,128,128]{2,1,0:T(8,128)(2,1)}, bf16[6,128,128]{2,1,0:T(8,128)(2,1)}, u32[]{:S(2)}, u32[]{:S(2)}) collective-permute-start(bf16[6,128,128]{2,1,0:T(8,128)(2,1)} %get-tuple-element.24), channel_id=1, source_target_pairs={{0,97},{1,33},{2,226},{3,34},{8,225},{9,161},{10,162},{11,98},{16,... | collective-permute-start | bytes 589832 | tf_op jit(solution)/shard_map/ppermute | solution.py:268
  11.9 2.4 %collective-permute-start.2 = (bf16[12,128,128]{2,1,0:T(8,128)(2,1)}, bf16[12,128,128]{2,1,0:T(8,128)(2,1)}, u32[]{:S(2)}, u32[]{:S(2)}) collective-permute-start(bf16[12,128,128]{2,1,0:T(8,128)(2,1)} %get-tuple-element.21), channel_id=1, source_target_pairs={{0,192},{1,1},{2,129},{7,0},{8,128},{9,65},{10,193},{15,64},{16,44... | collective-permute-start | bytes 1179656 | tf_op jit(solution)/shard_map/ppermute | solution.py:267
  14.3 0.0 copy-start.2
  14.3 1.4 %constant_dynamic-slice_fusion = (bf16[2,384,384]{2,1,0:T(8,128)(2,1)S(1)}, bf16[2,384,384]{2,1,0:T(8,128)(2,1)S(1)}) fusion(bf16[2,768,384]{2,1,0:T(8,128)(2,1)} %field.3, s32[]{:T(128)S(6)} %select_n.17, s32[]{:T(128)S(6)} %select_n.16), kind=kLoop, calls=%fused_computation.3 | loop fusion | bytes 2359304 | tf_op jit(solution)/shard_map/dynamic_slice | solution.py:98
  15.7 0.0 copy-start
  15.7 0.0 copy-done.2
  15.8 1.3 %pad_maximum_fusion = (bf16[1024,384]{1,0:T(8,128)(2,1)}, bf16[1024,384]{1,0:T(8,128)(2,1)}) fusion(bf16[256,384]{1,0:T(8,128)(2,1)S(1)} %copy-done.2, bf16[768,384]{1,0:T(8,128)(2,1)S(1)} %bitcast.3, bf16[768,384]{1,0:T(8,128)(2,1)S(1)} %bitcast.4), kind=kLoop, calls=%fused_computation | loop fusion | flops 2752512 | bytes 2949120 | tf_op jit(solution)/shard_map/concatenate | solution.py:99
  17.1 7.8 %collective-permute-start.5 = (bf16[1024,384]{1,0:T(8,128)(2,1)}, bf16[1024,384]{1,0:T(8,128)(2,1)}, u32[]{:S(2)}, u32[]{:S(2)}) collective-permute-start(bf16[1024,384]{1,0:T(8,128)(2,1)} %get-tuple-element.36), channel_id=1, source_target_pairs={{32,64},{96,128},{160,192},{224,256},{288,320},{352,384},{416,448}... | collective-permute-start | bytes 2359304 | tf_op jit(solution)/shard_map/ppermute | solution.py:244
  24.9 0.0 collective-permute-done.3
  24.9 1.9 %collective-permute-start.6 = (bf16[1024,384]{1,0:T(8,128)(2,1)}, bf16[1024,384]{1,0:T(8,128)(2,1)}, u32[]{:S(2)}, u32[]{:S(2)}) collective-permute-start(bf16[1024,384]{1,0:T(8,128)(2,1)} %get-tuple-element.26), channel_id=1, source_target_pairs={{0,32},{32,0},{64,96},{96,64},{128,160},{160,128},{192,224},{224,1... | collective-permute-start | bytes 2359304 | tf_op jit(solution)/shard_map/ppermute | solution.py:239
  26.9 0.0 copy-done
  26.9 0.0 copy-start.1
  26.9 1.1 %copy-done.1 = bf16[24,128,128]{2,1,0:T(8,128)(2,1)S(1)} copy-done((bf16[24,128,128]{2,1,0:T(8,128)(2,1)S(1)}, bf16[24,128,128]{2,1,0:T(8,128)(2,1)}, u32[]{:S(2)}) %copy-start.1) | copy-done | bytes 786456
  28.0 1.2 %first_left.1 = (f32[2,768,384]{2,1,0:T(8,128)S(1)}, bf16[3,256,1024]{2,1,0:T(8,128)(2,1)S(1)}, bf16[384,384]{1,0:T(8,128)(2,1)S(1)}) custom-call(bf16[2,768,384]{2,1,0:T(8,128)(2,1)S(1)} %copy-done, bf16[24,128,128]{2,1,0:T(8,128)(2,1)S(1)} %copy-done.1), custom_call_target="tpu_custom_call" | custom-call | flops 1207959552 | bytes 8388608 | tf_op jit(solution)/shard_map/first_left/pallas_call | solution.py:269
  29.3 9.8 %collective-permute-done.2 = bf16[12,128,128]{2,1,0:T(8,128)(2,1)} collective-permute-done((bf16[12,128,128]{2,1,0:T(8,128)(2,1)}, bf16[12,128,128]{2,1,0:T(8,128)(2,1)}, u32[]{:S(2)}, u32[]{:S(2)}) %collective-permute-start.2) | collective-permute-done | bytes 393248 | tf_op jit(solution)/shard_map/ppermute | solution.py:267
  39.0 1.2 %maximum_select_fusion.halves = bf16[12,128,128]{2,1,0:T(8,128)(2,1)S(1)} fusion(bf16[12,128,128]{2,1,0:T(8,128)(2,1)} %collective-permute-done.2, bf16[6,128,128]{2,1,0:T(8,128)(2,1)} %collective-permute-done.3, pred[]{:T(512)S(6)} %eq.3), kind=kLoop, calls=%fused_computation.2 | loop fusion | flops 393216 | bytes 983041 | tf_op jit(solution)/shard_map/jit(_where)/select_n | solution.py:283
  40.2 1.9 %collective-permute-start.4 = (bf16[12,128,128]{2,1,0:T(8,128)(2,1)S(1)}, bf16[12,128,128]{2,1,0:T(8,128)(2,1)S(1)}, u32[]{:S(2)}, u32[]{:S(2)}) collective-permute-start(bf16[12,128,128]{2,1,0:T(8,128)(2,1)S(1)} %maximum_select_fusion.halves), channel_id=1, source_target_pairs={{0,32},{32,0},{64,96},{96,64},{128,160},{160,128},{192,224},{224,1... | collective-permute-start | bytes 1179656 | tf_op jit(solution)/shard_map/ppermute | solution.py:239
  42.2 1.7 %collective-permute-done.4.across = bf16[12,128,128]{2,1,0:T(8,128)(2,1)S(1)} collective-permute-done((bf16[12,128,128]{2,1,0:T(8,128)(2,1)S(1)}, bf16[12,128,128]{2,1,0:T(8,128)(2,1)S(1)}, u32[]{:S(2)}, u32[]{:S(2)}) %collective-permute-start.4) | collective-permute-done | bytes 393248 | tf_op jit(solution)/shard_map/ppermute | solution.py:239
  43.9 0.2 right_band.1.band
  44.1 10.6 %collective-permute-done.5.from_chip = bf16[1024,384]{1,0:T(8,128)(2,1)} collective-permute-done((bf16[1024,384]{1,0:T(8,128)(2,1)}, bf16[1024,384]{1,0:T(8,128)(2,1)}, u32[]{:S(2)}, u32[]{:S(2)}) %collective-permute-start.5) | collective-permute-done | bytes 786464 | tf_op jit(solution)/shard_map/ppermute | solution.py:244
  54.7 0.0 collective-permute-done.6.from_core
  54.7 0.0 collective-permute-done.1.after
  54.7 0.0 collective-permute-done.before
  54.7 4.3 %first_right.1 = (bf16[2,768,384]{2,1,0:T(8,128)(2,1)S(1)}, f32[2,768,384]{2,1,0:T(8,128)S(1)}, bf16[2,384,384]{2,1,0:T(8,128)(2,1)S(1)}, bf16[2,384,384]{2,1,0:T(8,128)(2,1)S(1)}, bf16[384,384]{1,0:T(8,128)(2,1)S(1)}) custom-call(bf16[2,768,384]{2,1,0:T(8,128)(2,1)S(1)} %collective-permute-done.before, bf16[2,768,384]{2,1,0:T(8,128)(2,1)S(1)} %copy-done, ...), custom_call_target="tpu_custom_call" | custom-call | flops 1358954496 | bytes 14680064 | tf_op jit(solution)/shard_map/first_right/pallas_call | solution.py:297
  59.0 1.9 %collective-permute-start.8 = (bf16[2,768,384]{2,1,0:T(8,128)(2,1)S(1)}, bf16[2,768,384]{2,1,0:T(8,128)(2,1)S(1)}, u32[]{:S(2)}, u32[]{:S(2)}) collective-permute-start(bf16[2,768,384]{2,1,0:T(8,128)(2,1)S(1)} %get-tuple-element.28.middle), channel_id=1, source_target_pairs={{1,0},{2,1},{3,2},{4,3},{5,4},{6,5},{7,6},{8,7},{9,8},{10,9},{11,1... | collective-permute-start | bytes 3538952 | tf_op jit(solution)/shard_map/ppermute | solution.py:41
  60.9 6.0 %collective-permute-start.7 = (bf16[2,768,384]{2,1,0:T(8,128)(2,1)S(1)}, bf16[2,768,384]{2,1,0:T(8,128)(2,1)S(1)}, u32[]{:S(2)}, u32[]{:S(2)}) collective-permute-start(bf16[2,768,384]{2,1,0:T(8,128)(2,1)S(1)} %get-tuple-element.28.middle), channel_id=1, source_target_pairs={{0,1},{1,2},{2,3},{3,4},{4,5},{5,6},{6,7},{7,8},{8,9},{9,10},{10,1... | collective-permute-start | bytes 3538952 | tf_op jit(solution)/shard_map/ppermute | solution.py:41
  67.0 4.6 %collective-permute-start.9 = (bf16[2,384,384]{2,1,0:T(8,128)(2,1)S(1)}, bf16[2,384,384]{2,1,0:T(8,128)(2,1)S(1)}, u32[]{:S(2)}, u32[]{:S(2)}) collective-permute-start(bf16[2,384,384]{2,1,0:T(8,128)(2,1)S(1)} %get-tuple-element.30), channel_id=1, source_target_pairs={{32,64},{96,128},{160,192},{224,256},{288,320},{352,384},{416,448}... | collective-permute-start | bytes 1769480 | tf_op jit(solution)/shard_map/ppermute | solution.py:244
  71.6 1.9 %collective-permute-start.10 = (bf16[2,384,384]{2,1,0:T(8,128)(2,1)S(1)}, bf16[2,384,384]{2,1,0:T(8,128)(2,1)S(1)}, u32[]{:S(2)}, u32[]{:S(2)}) collective-permute-start(bf16[2,384,384]{2,1,0:T(8,128)(2,1)S(1)} %get-tuple-element.31), channel_id=1, source_target_pairs={{0,32},{32,0},{64,96},{96,64},{128,160},{160,128},{192,224},{224,1... | collective-permute-start | bytes 1769480 | tf_op jit(solution)/shard_map/ppermute | solution.py:239
  73.5 1.8 %second_left.1.total = f32[2,768,384]{2,1,0:T(8,128)S(1)} custom-call(bf16[2,768,384]{2,1,0:T(8,128)(2,1)S(1)} %get-tuple-element.28.middle, bf16[3,256,1024]{2,1,0:T(8,128)(2,1)S(1)} %get-tuple-element.22.band, bf16[1152,384]{1,0:T(8,128)(2,1)S(1)} %right_band.1.band, f32[2,768,384]{2,1,0:T(8,128)S(1)} %get-tuple-element.29.total), custom_call_target="tpu_custom_call" | custom-call | flops 1660944384 | bytes 10485760 | tf_op jit(solution)/shard_map/second_left/pallas_call | solution.py:317
  75.3 28.1 %collective-permute-done.9.from_chip = bf16[2,384,384]{2,1,0:T(8,128)(2,1)S(1)} collective-permute-done((bf16[2,384,384]{2,1,0:T(8,128)(2,1)S(1)}, bf16[2,384,384]{2,1,0:T(8,128)(2,1)S(1)}, u32[]{:S(2)}, u32[]{:S(2)}) %collective-permute-start.9) | collective-permute-done | bytes 589856 | tf_op jit(solution)/shard_map/ppermute | solution.py:244
  103.4 0.0 collective-permute-done.10.from_core
  103.4 0.0 collective-permute-done.8.after
  103.4 0.0 collective-permute-done.7.before
  103.4 3.2 %last.1 = f32[2,768,384]{2,1,0:T(8,128)} custom-call(bf16[2,768,384]{2,1,0:T(8,128)(2,1)S(1)} %collective-permute-done.7.before, bf16[2,768,384]{2,1,0:T(8,128)(2,1)S(1)} %collective-permute-done.8.after, f32[2,768,384]{2,1,0:T(8,128)S(1)} %second_left.1.total, bf16[1152,384]{1,0:T(8,128)(2,1)S(1)} %right_band.1.band, ...), custom_call_target="tpu_custom_call" | custom-call | flops 905969664 | bytes 8388608 | tf_op jit(solution)/shard_map/last/pallas_call | solution.py:326
Async XLA Ops:
  0.0 54.7 %collective-permute-start.1 = (bf16[2,768,384]{2,1,0:T(8,128)(2,1)}, bf16[2,768,384]{2,1,0:T(8,128)(2,1)S(1)}, u32[]{:S(2)}, u32[]{:S(2)}) collective-permute-start(bf16[2,768,384]{2,1,0:T(8,128)(2,1)} %field.3), channel_id=1, source_target_pairs={{1,0},{2,1},{3,2},{4,3},{5,4},{6,5},{7,6},{8,7},{9,8},{10,9},{11,1... | collective-permute-start | bytes 3538952 | tf_op jit(solution)/shard_map/ppermute | solution.py:41
  2.5 52.3 %collective-permute-start = (bf16[2,768,384]{2,1,0:T(8,128)(2,1)}, bf16[2,768,384]{2,1,0:T(8,128)(2,1)S(1)}, u32[]{:S(2)}, u32[]{:S(2)}) collective-permute-start(bf16[2,768,384]{2,1,0:T(8,128)(2,1)} %field.3), channel_id=1, source_target_pairs={{0,1},{1,2},{2,3},{3,4},{4,5},{5,6},{6,7},{7,8},{8,9},{9,10},{10,1... | collective-permute-start | bytes 3538952 | tf_op jit(solution)/shard_map/ppermute | solution.py:41
  10.5 14.4 %collective-permute-start.3 = (bf16[6,128,128]{2,1,0:T(8,128)(2,1)}, bf16[6,128,128]{2,1,0:T(8,128)(2,1)}, u32[]{:S(2)}, u32[]{:S(2)}) collective-permute-start(bf16[6,128,128]{2,1,0:T(8,128)(2,1)} %get-tuple-element.24), channel_id=1, source_target_pairs={{0,97},{1,33},{2,226},{3,34},{8,225},{9,161},{10,162},{11,98},{16,... | collective-permute-start | bytes 589832 | tf_op jit(solution)/shard_map/ppermute | solution.py:268
  11.9 27.2 %collective-permute-start.2 = (bf16[12,128,128]{2,1,0:T(8,128)(2,1)}, bf16[12,128,128]{2,1,0:T(8,128)(2,1)}, u32[]{:S(2)}, u32[]{:S(2)}) collective-permute-start(bf16[12,128,128]{2,1,0:T(8,128)(2,1)} %get-tuple-element.21), channel_id=1, source_target_pairs={{0,192},{1,1},{2,129},{7,0},{8,128},{9,65},{10,193},{15,64},{16,44... | collective-permute-start | bytes 1179656 | tf_op jit(solution)/shard_map/ppermute | solution.py:267
  14.3 1.4 %copy-start.2 = (bf16[256,384]{1,0:T(8,128)(2,1)S(1)}, bf16[256,384]{1,0:T(8,128)(2,1)}, u32[]{:S(2)}) copy-start(bf16[256,384]{1,0:T(8,128)(2,1)} %get-tuple-element.25) | copy-start | bytes 589828
  15.7 11.1 %copy-start = (bf16[2,768,384]{2,1,0:T(8,128)(2,1)S(1)}, bf16[2,768,384]{2,1,0:T(8,128)(2,1)}, u32[]{:S(2)}) copy-start(bf16[2,768,384]{2,1,0:T(8,128)(2,1)} %field.3) | copy-start | bytes 3538948
  17.1 37.6 %collective-permute-start.5 = (bf16[1024,384]{1,0:T(8,128)(2,1)}, bf16[1024,384]{1,0:T(8,128)(2,1)}, u32[]{:S(2)}, u32[]{:S(2)}) collective-permute-start(bf16[1024,384]{1,0:T(8,128)(2,1)} %get-tuple-element.36), channel_id=1, source_target_pairs={{32,64},{96,128},{160,192},{224,256},{288,320},{352,384},{416,448}... | collective-permute-start | bytes 2359304 | tf_op jit(solution)/shard_map/ppermute | solution.py:244
  24.9 29.8 %collective-permute-start.6 = (bf16[1024,384]{1,0:T(8,128)(2,1)}, bf16[1024,384]{1,0:T(8,128)(2,1)}, u32[]{:S(2)}, u32[]{:S(2)}) collective-permute-start(bf16[1024,384]{1,0:T(8,128)(2,1)} %get-tuple-element.26), channel_id=1, source_target_pairs={{0,32},{32,0},{64,96},{96,64},{128,160},{160,128},{192,224},{224,1... | collective-permute-start | bytes 2359304 | tf_op jit(solution)/shard_map/ppermute | solution.py:239
  26.9 1.1 %copy-start.1 = (bf16[24,128,128]{2,1,0:T(8,128)(2,1)S(1)}, bf16[24,128,128]{2,1,0:T(8,128)(2,1)}, u32[]{:S(2)}) copy-start(bf16[24,128,128]{2,1,0:T(8,128)(2,1)} %get-tuple-element.19.upper) | copy-start | bytes 2359300
  40.2 3.6 %collective-permute-start.4 = (bf16[12,128,128]{2,1,0:T(8,128)(2,1)S(1)}, bf16[12,128,128]{2,1,0:T(8,128)(2,1)S(1)}, u32[]{:S(2)}, u32[]{:S(2)}) collective-permute-start(bf16[12,128,128]{2,1,0:T(8,128)(2,1)S(1)} %maximum_select_fusion.halves), channel_id=1, source_target_pairs={{0,32},{32,0},{64,96},{96,64},{128,160},{160,128},{192,224},{224,1... | collective-permute-start | bytes 1179656 | tf_op jit(solution)/shard_map/ppermute | solution.py:239
  59.0 44.4 %collective-permute-start.8 = (bf16[2,768,384]{2,1,0:T(8,128)(2,1)S(1)}, bf16[2,768,384]{2,1,0:T(8,128)(2,1)S(1)}, u32[]{:S(2)}, u32[]{:S(2)}) collective-permute-start(bf16[2,768,384]{2,1,0:T(8,128)(2,1)S(1)} %get-tuple-element.28.middle), channel_id=1, source_target_pairs={{1,0},{2,1},{3,2},{4,3},{5,4},{6,5},{7,6},{8,7},{9,8},{10,9},{11,1... | collective-permute-start | bytes 3538952 | tf_op jit(solution)/shard_map/ppermute | solution.py:41
  60.9 42.5 %collective-permute-start.7 = (bf16[2,768,384]{2,1,0:T(8,128)(2,1)S(1)}, bf16[2,768,384]{2,1,0:T(8,128)(2,1)S(1)}, u32[]{:S(2)}, u32[]{:S(2)}) collective-permute-start(bf16[2,768,384]{2,1,0:T(8,128)(2,1)S(1)} %get-tuple-element.28.middle), channel_id=1, source_target_pairs={{0,1},{1,2},{2,3},{3,4},{4,5},{5,6},{6,7},{7,8},{8,9},{9,10},{10,1... | collective-permute-start | bytes 3538952 | tf_op jit(solution)/shard_map/ppermute | solution.py:41
  67.0 36.5 %collective-permute-start.9 = (bf16[2,384,384]{2,1,0:T(8,128)(2,1)S(1)}, bf16[2,384,384]{2,1,0:T(8,128)(2,1)S(1)}, u32[]{:S(2)}, u32[]{:S(2)}) collective-permute-start(bf16[2,384,384]{2,1,0:T(8,128)(2,1)S(1)} %get-tuple-element.30), channel_id=1, source_target_pairs={{32,64},{96,128},{160,192},{224,256},{288,320},{352,384},{416,448}... | collective-permute-start | bytes 1769480 | tf_op jit(solution)/shard_map/ppermute | solution.py:244
  71.6 31.9 %collective-permute-start.10 = (bf16[2,384,384]{2,1,0:T(8,128)(2,1)S(1)}, bf16[2,384,384]{2,1,0:T(8,128)(2,1)S(1)}, u32[]{:S(2)}, u32[]{:S(2)}) collective-permute-start(bf16[2,384,384]{2,1,0:T(8,128)(2,1)S(1)} %get-tuple-element.31), channel_id=1, source_target_pairs={{0,32},{32,0},{64,96},{96,64},{128,160},{160,128},{192,224},{224,1... | collective-permute-start | bytes 1769480 | tf_op jit(solution)/shard_map/ppermute | solution.py:239
